TPU v7x, 32 devices: a whole 2x2x4 slice. The times are simulated.
32 devices in a mesh: ctx: 8 (over z, x), tp: 4 (over y, core).
Axes of the slice: x: 2, y: 2, z: 4, core: 2. Of those that a mesh axis runs over, the one named last changes fastest.
Arguments:
- tokens: bfloat16 [2048, 2048], P(('ctx', 'tp')), may hold values from -6 to 6
- w_query_key: bfloat16 [2, 2048, 2048], P(None, None, 'tp'), may hold values from -0.125 to 0.125
- w_value: bfloat16 [2048, 4096], P(None, 'tp'), may hold values from -0.125 to 0.125
- w_gate_out: bfloat16 [2048, 4096], P(None, 'tp'), may hold values from -0.125 to 0.125
- conv_query_key: float32 [2, 4, 2048], P(None, None, 'tp'), may hold values from -3 to 3
- conv_value: float32 [4, 4096], P(None, 'tp'), may hold values from -3 to 3
- log_decay: float32 [32, 2048], P('tp', 'ctx'), as said below
- beta: float32 [32, 2048], P('tp', 'ctx'), as said below
- seg_start: int32 [2048], P('ctx'), may hold values from 0 to 2047, as said below
- norm_gain: float32 [128], replicated, may hold values from 0.1 to 1.9
- w_output: bfloat16 [4096, 2048], P('tp'), may hold values from -0.09375 to 0.09375
Outputs:
- mixed: bfloat16 [2048, 2048], P(('ctx', 'tp'))
Inputs may be any that keep to these rules, and one draw needn't show every extreme that they name: seg_start never falls along the tokens, seg_start[t] <= t, and seg_start[t] == t exactly at the first token of each rollout; two to five rollouts, the last token opening one of its own. log_decay <= 0. 0 < beta < 1.
All inputs are finite; a program needn't handle non-finite values.
Results may differ from a plain program's by a relative error of at most 0.014.
Values may be sent and summed in bfloat16 or wider, within the bound.
A program may use at most 64 MiB of HBM per device.

v0:
```python
import jax
import jax.numpy as jnp
from jax import lax
from jax.sharding import PartitionSpec as P

HK = 16
DK = 128
VALUE_HEADS = 32
DV = 128
CONV = 4
STRETCH = 64


highest = lax.Precision.HIGHEST


def passed_along(array, axis, by):
    devices = lax.axis_size(axis)
    pairs = [(i, i + by) for i in range(devices) if 0 <= i + by < devices]
    return lax.ppermute(array, axis, pairs)


def stretch_parts(query, key, value, logd, betas, segs, first):
    size = segs.shape[0]
    gam = jnp.cumsum(logd, axis=-1)
    rows = jnp.arange(size)[:, None]
    cols = jnp.arange(size)[None, :]
    same = segs[:, None] == segs[None, :]
    within = jnp.logical_and(rows >= cols, same)
    strict = jnp.logical_and(rows > cols, same)
    gap = gam[:, :, None] - gam[:, None, :]
    decay = jnp.where(within, jnp.exp(jnp.where(within, gap, 0.0)), 0.0)
    lead = jnp.exp(gam) * (segs < first).astype(jnp.float32)
    keys_dot = jnp.einsum("hid,hjd->hij", key, key, precision=highest)
    lower_mat = jnp.eye(size, dtype=jnp.float32) + betas[:, :, None] * keys_dot * jnp.where(
        strict, decay, 0.0
    )
    w_one = lax.linalg.triangular_solve(
        lower_mat, betas[:, :, None] * value, left_side=True, lower=True, unit_diagonal=True
    )
    w_two = lax.linalg.triangular_solve(
        lower_mat, (betas * lead)[:, :, None] * key, left_side=True, lower=True, unit_diagonal=True
    )
    pmat = jnp.einsum("hid,hjd->hij", query, key, precision=highest) * decay
    local_out = jnp.einsum("hij,hjv->hiv", pmat, w_one, precision=highest)
    edge = lead[:, :, None] * query - jnp.einsum("hij,hjd->hid", pmat, w_two, precision=highest)
    tail = decay[:, -1, :]
    eye_key = jnp.eye(key.shape[-1], dtype=jnp.float32)
    mmat = lead[:, -1][:, None, None] * eye_key - jnp.einsum(
        "hj,hjd,hje->hde", tail, w_two, key, precision=highest
    )
    bmat = jnp.einsum("hj,hjv,hjk->hvk", tail, w_one, key, precision=highest)
    return (local_out, edge, mmat, bmat)


def short_conv(pre, tail, weight, seg, position):
    extended = jnp.concatenate([tail, pre], axis=0).astype(jnp.float32)
    count = pre.shape[0]
    total = jnp.zeros((count, pre.shape[1]), jnp.float32)
    for j in range(CONV):
        reach = position - (CONV - 1) + j
        valid = (reach >= seg).astype(jnp.float32)[:, None]
        total = total + extended[j : j + count] * weight[j][None, :] * valid
    return jax.nn.silu(total)


def unit_norm(vecs):
    return vecs * lax.rsqrt(jnp.sum(vecs * vecs, axis=-1, keepdims=True) + 1e-06)


def compose_maps(earlier, later):
    return (
        jnp.einsum("hab,hbc->hac", earlier[0], later[0], precision=highest),
        jnp.einsum("hvb,hbc->hvc", earlier[1], later[0], precision=highest) + later[1],
    )


def local(
    tokens,
    w_query_key,
    w_value,
    w_gate_out,
    conv_query_key,
    conv_value,
    log_decay,
    beta,
    seg_start,
    norm_gain,
    w_output,
):
    width_qk = w_query_key.shape[2]
    width_v = w_value.shape[1]
    heads_k = width_qk // DK
    heads_v = width_v // DV
    count = seg_start.shape[0]
    piece = lax.all_gather(tokens, "tp", axis=0, tiled=True)
    projected = jnp.concatenate(
        [
            jnp.dot(piece, w_query_key[0], preferred_element_type=jnp.float32),
            jnp.dot(piece, w_query_key[1], preferred_element_type=jnp.float32),
            jnp.dot(piece, w_value, preferred_element_type=jnp.float32),
            jnp.dot(piece, w_gate_out, preferred_element_type=jnp.float32),
        ],
        axis=1,
    )
    split_at = 2 * width_qk + width_v
    pre = projected[:, :split_at].astype(jnp.bfloat16)
    gate_lin = projected[:, split_at:]
    received_tail = passed_along(pre[count - (CONV - 1) :], "ctx", 1)
    taps = jnp.concatenate([conv_query_key[0], conv_query_key[1], conv_value], axis=1)
    offset = lax.axis_index("ctx") * count
    position = offset + jnp.arange(count)
    act = short_conv(pre, received_tail, taps, seg_start, position)
    query = unit_norm(act[:, :width_qk].reshape(count, heads_k, DK)) * DK ** (-0.5)
    key = unit_norm(act[:, width_qk : 2 * width_qk].reshape(count, heads_k, DK))
    value = act[:, 2 * width_qk :].reshape(count, heads_v, DV)
    repeat = VALUE_HEADS // HK
    query = jnp.repeat(query, repeat, axis=1)
    key = jnp.repeat(key, repeat, axis=1)
    blocks = count // STRETCH

    def arrange(field, depth):
        return field.reshape(blocks, STRETCH, heads_v, depth).transpose(0, 2, 1, 3)

    logd = log_decay.reshape(heads_v, blocks, STRETCH).transpose(1, 0, 2)
    betas = beta.reshape(heads_v, blocks, STRETCH).transpose(1, 0, 2)
    segs = seg_start.reshape(blocks, STRETCH)
    firsts = offset + jnp.arange(blocks) * STRETCH
    local_out, edge, mmat, bmat = jax.vmap(stretch_parts)(
        arrange(query, DK), arrange(key, DK), arrange(value, DV), logd, betas, segs, firsts
    )
    eye_maps = jnp.broadcast_to(jnp.eye(DK, dtype=jnp.float32), (heads_v, DK, DK))
    zero_state = jnp.zeros((heads_v, DV, DK), jnp.float32)

    def fold_block(acc, pieces):
        return (compose_maps(acc, pieces), None)

    (shard_map_m, shard_map_b), _ = lax.scan(fold_block, (eye_maps, zero_state), (mmat, bmat))

    def turn(index, incoming):
        outgoing = (
            jnp.einsum("hvk,hkl->hvl", incoming, shard_map_m, precision=highest) + shard_map_b
        )
        return passed_along(outgoing, "ctx", 1)

    state_in = lax.fori_loop(0, lax.axis_size("ctx") - 1, turn, zero_state)

    def advance(state, pieces):
        out_blk, edge_blk, m_blk, b_blk = pieces
        result = out_blk + jnp.einsum("hik,hvk->hiv", edge_blk, state, precision=highest)
        state = jnp.einsum("hvk,hkl->hvl", state, m_blk, precision=highest) + b_blk
        return (state, result)

    _, results = lax.scan(advance, state_in, (local_out, edge, mmat, bmat))
    recur_out = results.transpose(0, 2, 1, 3).reshape(count, heads_v, DV)
    scale = lax.rsqrt(jnp.mean(recur_out * recur_out, axis=-1, keepdims=True) + 1e-06)
    normed = recur_out * scale * norm_gain * jax.nn.silu(gate_lin.reshape(count, heads_v, DV))
    normed = normed.reshape(count, width_v).astype(jnp.bfloat16)
    return lax.psum_scatter(
        jnp.dot(normed, w_output, preferred_element_type=jnp.float32).astype(jnp.bfloat16),
        "tp",
        scatter_dimension=0,
        tiled=True,
    )


def solution(mesh):
    return jax.shard_map(
        local,
        mesh=mesh,
        in_specs=(
            P(("ctx", "tp"), None),
            P(None, None, "tp"),
            P(None, "tp"),
            P(None, "tp"),
            P(None, None, "tp"),
            P(None, "tp"),
            P("tp", "ctx"),
            P("tp", "ctx"),
            P("ctx"),
            P(),
            P("tp", None),
        ),
        out_specs=P(("ctx", "tp"), None),
        check_vma=False,
    )
```

profile of v0, /device:TPU:24, one launch (start us, length us, event | category | flops | bytes accessed | tf_op | source)
XLA Modules:
  0.0 416.6 jit_solution(17867635439460446899)
XLA Ops:
  9.5 0.8 reshape.138
  10.3 0.8 reshape.140
  11.1 0.9 reduce_window_sum.11
  13.4 13.3 %all-gather.2.cloned.1.call-done = bf16[256,2048]{1,0:T(8,128)(2,1)} async-done(((bf16[64,2048]{1,0:T(8,128)(2,1)}), bf16[256,2048]{1,0:T(8,128)(2,1)}) %all-gather.2.cloned.1.call-update) | async-done | bytes 1048592 | tf_op jit(solution)/shard_map/all_gather | solution.py:96
  26.7 2.8 fusion.38
  29.8 2.1 fusion.41
  32.3 2.5 convolution_convert_fusion.1
  34.8 3.4 collective-permute-start.1
  38.5 2.8 collective-permute-done.1
  41.7 2.1 divide_multiply_fusion
  43.8 1.1 slice_bitcast_fusion
  47.0 1.0 copy-done.1
  48.0 1.8 convolution_multiply_fusion
  49.8 2.9 fusion.37
  52.7 158.7 %custom-call.5 = f32[4,8,1,64,64]{3,4,2,1,0:T(8,128)} custom-call(f32[4,8,1,64,64]{4,3,2,1,0:T(8,128)} %fusion.37), custom_call_target="InvertDiagBlocksLowerTriangular" | custom-call | tf_op jit(solution)/shard_map/vmap()/triangular_solve/custom-call.1 | solution.py:41
  211.4 1.5 copy.128
  212.9 2.1 fusion.50
  215.0 2.1 fusion.48
  217.1 2.3 convolution_subtract_fusion
  219.4 2.2 fusion.77
  221.6 5.2 %fusion.54 = f32[4,8,128,128]{2,3,1,0:T(8,128)} fusion(f32[4,8,64,128]{3,2,1,0:T(8,128)S(1)} %fusion.48, f32[4,8,64,128]{3,2,0,1:T(8,128)S(1)} %bitcast.157, f32[4,8,64]{2,1,0:T(8,128)S(1)} %bitcast.166), kind=kOutput, calls=%fused_computation.72 | convolution fusion | flops 402915328 | bytes 4202496 | tf_op jit(solution)/shard_map/vmap(hj,hjv,hjk->hvk)/dot_general | solution.py:52
  226.7 5.5 %multiply_subtract_fusion = f32[4,8,128,128]{3,2,1,0:T(8,128)} fusion(f32[4,8,64,128]{3,2,1,0:T(8,128)S(1)} %fusion.50, f32[128,128]{1,0:T(8,128)S(1)} %fusion.68, f32[4,8]{1,0:T(4,128)S(1)} %slice_reduce_fusion, f32[4,8,64,128]{3,2,0,1:T(8,128)S(1)} %bitcast.158, f32[4,8,64]{2,1,0:T(8,128)S(1)} %bitcast.167), kind=kOutput, calls=%fused_computation.44 | convolution fusion | flops 403963904 | bytes 4268160 | tf_op jit(solution)/shard_map/vmap(hj,hjd,hje->hde)/dot_general | solution.py:49
  232.2 1.9 copy.106
  234.2 10.0 %while.37 = (s32[]{:T(128)}, f32[8,128,128]{1,2,0:T(8,128)S(1)}, f32[8,128,128]{1,2,0:T(8,128)S(1)}, f32[4,8,128,128]{2,3,1,0:T(8,128)S(1)}, f32[4,8,128,128]{2,3,1,0:T(8,128)}, /*index=5*/s32[]{:T(128)}, s32[]{:T(128)}) while((s32[]{:T(128)}, f32[8,128,128]{1,2,0:T(8,128)S(1)}, f32[8,128,128]{1,2,0:T(8,128)S(1)}, ...), condition=%wide.region_3.5_spmd.clone, body=%wide.region_2.0_spmd.clone.sunk | while | flops 402915328 | bytes 5768283 | solution.py:138
  234.2 1.7 fusion.119
  236.7 1.7 fusion.119
  239.2 1.7 fusion.119
  241.7 1.7 fusion.119
  244.2 1.0 copy.108
  245.4 112.1 %while.35 = (s32[]{:T(128)}, f32[8,128,128]{2,1,0:T(8,128)S(1)}, f32[8,128,128]{2,1,0:T(8,128)}, f32[8,128,128]{2,1,0:T(8,128)S(1)}, s32[]{:T(128)}) while((s32[]{:T(128)}, f32[8,128,128]{2,1,0:T(8,128)S(1)}, f32[8,128,128]{2,1,0:T(8,128)}, f32[8,128,128]{2,1,0:T(8,128)S(1)}, s32[]{:T(128)}) %tuple.76), condition=%wide.region_5.7_spmd, body=%wide.region_4.6_spmd.sunk | while | flops 201457664 | bytes 4194405 | solution.py:146
  245.4 2.5 convolution_add_fusion.3
  247.9 2.5 collective-permute-start
  250.4 13.4 %collective-permute-done = f32[8,128,128]{2,1,0:T(8,128)S(1)} collective-permute-done((f32[8,128,128]{2,1,0:T(8,128)}, f32[8,128,128]{2,1,0:T(8,128)S(1)}, u32[]{:S(2)}, u32[]{:S(2)}) %collective-permute-start) | collective-permute-done | bytes 524320 | tf_op jit(solution)/shard_map/while/body/eval_jaxpr/ppermute | solution.py:20
  263.8 2.5 convolution_add_fusion.3
  266.3 1.9 collective-permute-start
  268.3 13.1 %collective-permute-done = f32[8,128,128]{2,1,0:T(8,128)S(1)} collective-permute-done((f32[8,128,128]{2,1,0:T(8,128)}, f32[8,128,128]{2,1,0:T(8,128)S(1)}, u32[]{:S(2)}, u32[]{:S(2)}) %collective-permute-start) | collective-permute-done | bytes 524320 | tf_op jit(solution)/shard_map/while/body/eval_jaxpr/ppermute | solution.py:20
  281.3 2.5 convolution_add_fusion.3
  283.8 1.9 collective-permute-start
  285.7 12.1 %collective-permute-done = f32[8,128,128]{2,1,0:T(8,128)S(1)} collective-permute-done((f32[8,128,128]{2,1,0:T(8,128)}, f32[8,128,128]{2,1,0:T(8,128)S(1)}, u32[]{:S(2)}, u32[]{:S(2)}) %collective-permute-start) | collective-permute-done | bytes 524320 | tf_op jit(solution)/shard_map/while/body/eval_jaxpr/ppermute | solution.py:20
  297.9 2.5 convolution_add_fusion.3
  300.4 1.9 collective-permute-start
  302.3 11.2 %collective-permute-done = f32[8,128,128]{2,1,0:T(8,128)S(1)} collective-permute-done((f32[8,128,128]{2,1,0:T(8,128)}, f32[8,128,128]{2,1,0:T(8,128)S(1)}, u32[]{:S(2)}, u32[]{:S(2)}) %collective-permute-start) | collective-permute-done | bytes 524320 | tf_op jit(solution)/shard_map/while/body/eval_jaxpr/ppermute | solution.py:20
  313.5 2.5 convolution_add_fusion.3
  316.0 1.9 collective-permute-start
  317.9 10.3 %collective-permute-done = f32[8,128,128]{2,1,0:T(8,128)S(1)} collective-permute-done((f32[8,128,128]{2,1,0:T(8,128)}, f32[8,128,128]{2,1,0:T(8,128)S(1)}, u32[]{:S(2)}, u32[]{:S(2)}) %collective-permute-start) | collective-permute-done | bytes 524320 | tf_op jit(solution)/shard_map/while/body/eval_jaxpr/ppermute | solution.py:20
  328.2 2.5 convolution_add_fusion.3
  330.7 1.9 collective-permute-start
  332.7 10.3 %collective-permute-done = f32[8,128,128]{2,1,0:T(8,128)S(1)} collective-permute-done((f32[8,128,128]{2,1,0:T(8,128)}, f32[8,128,128]{2,1,0:T(8,128)S(1)}, u32[]{:S(2)}, u32[]{:S(2)}) %collective-permute-start) | collective-permute-done | bytes 524320 | tf_op jit(solution)/shard_map/while/body/eval_jaxpr/ppermute | solution.py:20
  342.9 2.5 convolution_add_fusion.3
  345.4 1.9 collective-permute-start
  347.3 10.3 %collective-permute-done = f32[8,128,128]{2,1,0:T(8,128)S(1)} collective-permute-done((f32[8,128,128]{2,1,0:T(8,128)}, f32[8,128,128]{2,1,0:T(8,128)S(1)}, u32[]{:S(2)}, u32[]{:S(2)}) %collective-permute-start) | collective-permute-done | bytes 524320 | tf_op jit(solution)/shard_map/while/body/eval_jaxpr/ppermute | solution.py:20
  357.8 16.5 %while.36 = (s32[]{:T(128)}, f32[8,128,128]{1,2,0:T(8,128)S(1)}, f32[4,8,64,128]{3,2,1,0:T(8,128)}, f32[4,8,128,128]{2,3,1,0:T(8,128)S(1)}, f32[4,8,128,128]{2,3...) while((s32[]{:T(128)}, f32[8,128,128]{1,2,0:T(8,128)S(1)}, ...), condition=%wide.region_8.10_spmd, body=%wide.region_7.9_spmd.sunk | while | flops 302186496 | bytes 4458581 | solution.py:154
  357.8 2.4 fusion.114
  360.2 1.7 fusion.113
  362.0 2.3 fusion.114
  364.3 1.7 fusion.113
  366.1 2.3 fusion.114
  368.5 1.7 fusion.113
  370.2 2.3 fusion.114
  372.6 1.7 fusion.113
  374.3 1.6 multiply_reduce_fusion
  376.0 1.8 copy.116
  378.2 7.4 %convolution_convert_fusion = bf16[256,2048]{1,0:T(8,128)(2,1)} fusion(bf16[1024,2048]{1,0:T(8,128)(2,1)} %param.29, f32[32,8,8,128]{3,2,1,0:T(8,128)S(1)} %bitcast.163, f32[32,8,8,128]{3,2,1,0:T(8,128)S(1)} %bitcast.164, f32[1024]{0:T(1024)S(1)} %broadcast_bitcast_fusion, bf16[256,2048]{1,0:T(8,128)(2,1)} %all-gather.2.cloned.1.call-done, ...), kind=kOutput, calls=%fused_computation.25 | convolution fusion | flops 2150105088 | bytes 12587008 | tf_op jit(solution)/shard_map/dot_general | solution.py:160
  385.7 24.2 %reduce-scatter.2.cloned.1.call-done = bf16[64,2048]{1,0:T(8,128)(2,1)} async-done(((bf16[256,2048]{1,0:T(8,128)(2,1)}), bf16[64,2048]{1,0:T(8,128)(2,1)}) %reduce-scatter.2.cloned.1.call-update) | async-done | bytes 262160 | tf_op jit(solution)/shard_map/reduce_scatter | solution.py:159
  (77 shorter events, 11.8 us)
Async XLA Ops:
  6.5 4.6 %copy-start = (f32[128]{0:T(128)S(1)}, f32[128]{0:T(128)}, u32[]{:S(2)}) copy-start(f32[128]{0:T(128)} %param.28) | copy-start | bytes 1540
  6.5 20.1 %all-gather.2.cloned.1.call-start = ((), (), s32[]{:S(2)}) async-start(), calls=%async_computation.1 | async-start | bytes 1310720 | tf_op jit(solution)/shard_map/all_gather | solution.py:96
  7.3 402.5 %reduce-scatter.2.cloned.1.call-start = ((), (), s32[]{:S(2)}) async-start(), calls=%async_computation.2 | async-start | bytes 1310720 | tf_op jit(solution)/shard_map/reduce_scatter | solution.py:159
  26.7 3.1 copy-start.4
  29.8 2.5 copy-start.5
  34.8 6.5 %collective-permute-start.1 = (bf16[3,2048]{1,0:T(4,128)(2,1)S(1)}, bf16[3,2048]{1,0:T(4,128)(2,1)S(1)}, u32[]{:S(2)}, u32[]{:S(2)}) collective-permute-start(bf16[3,2048]{1,0:T(4,128)(2,1)S(1)} %pad_maximum_fusion.1), channel_id=1, source_target_pairs={{0,4},{4,8},{8,12},{12,16},{16,20},{20,24},{24,28},{1,5},{5,9},{9,... | collective-permute-start | bytes 36872 | tf_op jit(solution)/shard_map/ppermute | solution.py:20
  47.0 1.0 copy-start.1
  211.4 1.5 copy-start.3
  215.0 2.1 copy-start.2
  247.9 15.9 %collective-permute-start = (f32[8,128,128]{2,1,0:T(8,128)}, f32[8,128,128]{2,1,0:T(8,128)S(1)}, u32[]{:S(2)}, u32[]{:S(2)}) collective-permute-start(f32[8,128,128]{2,1,0:T(8,128)} %convolution_add_fusion.3), channel_id=1, source_target_pairs={{0,4},{4,8},{8,12},{12,16},{16,20},{20,24},{24,28},{1,5},{5,9},{9,... | collective-permute-start | bytes 1572872 | tf_op jit(solution)/shard_map/while/body/eval_jaxpr/ppermute | solution.py:20
  266.3 15.0 %collective-permute-start = (f32[8,128,128]{2,1,0:T(8,128)}, f32[8,128,128]{2,1,0:T(8,128)S(1)}, u32[]{:S(2)}, u32[]{:S(2)}) collective-permute-start(f32[8,128,128]{2,1,0:T(8,128)} %convolution_add_fusion.3), channel_id=1, source_target_pairs={{0,4},{4,8},{8,12},{12,16},{16,20},{20,24},{24,28},{1,5},{5,9},{9,... | collective-permute-start | bytes 1572872 | tf_op jit(solution)/shard_map/while/body/eval_jaxpr/ppermute | solution.py:20
  283.8 14.1 %collective-permute-start = (f32[8,128,128]{2,1,0:T(8,128)}, f32[8,128,128]{2,1,0:T(8,128)S(1)}, u32[]{:S(2)}, u32[]{:S(2)}) collective-permute-start(f32[8,128,128]{2,1,0:T(8,128)} %convolution_add_fusion.3), channel_id=1, source_target_pairs={{0,4},{4,8},{8,12},{12,16},{16,20},{20,24},{24,28},{1,5},{5,9},{9,... | collective-permute-start | bytes 1572872 | tf_op jit(solution)/shard_map/while/body/eval_jaxpr/ppermute | solution.py:20
  300.4 13.1 %collective-permute-start = (f32[8,128,128]{2,1,0:T(8,128)}, f32[8,128,128]{2,1,0:T(8,128)S(1)}, u32[]{:S(2)}, u32[]{:S(2)}) collective-permute-start(f32[8,128,128]{2,1,0:T(8,128)} %convolution_add_fusion.3), channel_id=1, source_target_pairs={{0,4},{4,8},{8,12},{12,16},{16,20},{20,24},{24,28},{1,5},{5,9},{9,... | collective-permute-start | bytes 1572872 | tf_op jit(solution)/shard_map/while/body/eval_jaxpr/ppermute | solution.py:20
  316.0 12.2 %collective-permute-start = (f32[8,128,128]{2,1,0:T(8,128)}, f32[8,128,128]{2,1,0:T(8,128)S(1)}, u32[]{:S(2)}, u32[]{:S(2)}) collective-permute-start(f32[8,128,128]{2,1,0:T(8,128)} %convolution_add_fusion.3), channel_id=1, source_target_pairs={{0,4},{4,8},{8,12},{12,16},{16,20},{20,24},{24,28},{1,5},{5,9},{9,... | collective-permute-start | bytes 1572872 | tf_op jit(solution)/shard_map/while/body/eval_jaxpr/ppermute | solution.py:20
  330.7 12.2 %collective-permute-start = (f32[8,128,128]{2,1,0:T(8,128)}, f32[8,128,128]{2,1,0:T(8,128)S(1)}, u32[]{:S(2)}, u32[]{:S(2)}) collective-permute-start(f32[8,128,128]{2,1,0:T(8,128)} %convolution_add_fusion.3), channel_id=1, source_target_pairs={{0,4},{4,8},{8,12},{12,16},{16,20},{20,24},{24,28},{1,5},{5,9},{9,... | collective-permute-start | bytes 1572872 | tf_op jit(solution)/shard_map/while/body/eval_jaxpr/ppermute | solution.py:20
  345.4 12.2 %collective-permute-start = (f32[8,128,128]{2,1,0:T(8,128)}, f32[8,128,128]{2,1,0:T(8,128)S(1)}, u32[]{:S(2)}, u32[]{:S(2)}) collective-permute-start(f32[8,128,128]{2,1,0:T(8,128)} %convolution_add_fusion.3), channel_id=1, source_target_pairs={{0,4},{4,8},{8,12},{12,16},{16,20},{20,24},{24,28},{1,5},{5,9},{9,... | collective-permute-start | bytes 1572872 | tf_op jit(solution)/shard_map/while/body/eval_jaxpr/ppermute | solution.py:20
Sparse Core Ops, SparseCore 0:
  8.9 17.6 all-gather.1
  385.8 23.9 reduce-scatter.1
where the time goes:
time: 420 us; the launch traced here: 417 us
  other arithmetic  167 us (40%)
  waiting for transfers between devices  122 us (29%)
  matrix products  82.1 us (20%)
  starting transfers between devices  17.3 us (4%)
  local copies, waits for them, and re-layouts  14.4 us (3%)
  between operations  13.8 us (3%)
    another operation x4, other arithmetic, stretch_parts(): lax.linalg.triangular_solve(lower_mat, (betas * lead)[:, :, None] * key,...  159 us
    ppermute x8, waiting for transfers between devices, passed_along(): return lax.ppermute(array, axis, pairs)  83.5 us
    reduce_scatter x1, waiting for transfers between devices, local(): lax.psum_scatter(jnp.dot(normed, w_output, preferred_element_type=jnp.flo...  24.2 us
    dot_general x7, matrix products, turn(): jnp.einsum('hvk,hkl->hvl', incoming, shard_map_m, precision=highest)  17.5 us
    ppermute x8, starting transfers between devices, passed_along(): return lax.ppermute(array, axis, pairs)  17.3 us
    all_gather x1, waiting for transfers between devices, local(): piece = lax.all_gather(tokens, 'tp', axis=0, tiled=True)  13.3 us
    dot_general x4, matrix products, advance(): jnp.einsum('hik,hvk->hiv', edge_blk, state, precision=highest)  9.38 us
  transfers between devices with their start and end apart: 10, of which 10 were waited for; matrix products, arithmetic and copies ran while one was open for 2% of the time, Pallas kernels for 0%

commit v1 on v0

v1 whole, which is shorter than its diff:
```python
import functools

import jax
import jax.numpy as jnp
from jax import lax
from jax.experimental import pallas as pl
from jax.experimental.pallas import tpu as pltpu
from jax.sharding import PartitionSpec as P

DK = 128
DV = 128
CONV = 4
TAIL = 16
HALF = 128

MESH = pl.DeviceIdType.MESH
F32 = jnp.float32
BF16 = jnp.bfloat16


def mm(a, b, dims=((1,), (0,))):
    return lax.dot_general(a, b, (dims, ((), ())), preferred_element_type=F32)


def halves(a):
    high = a.astype(BF16)
    return high, (a - high.astype(F32)).astype(BF16)


def mm3(a, b):
    a_high, a_low = halves(a)
    b_high, b_low = halves(b)
    return mm(a_high, b_high) + (mm(a_high, b_low) + mm(a_low, b_high))


def column(row):
    return jnp.broadcast_to(row, (8, row.shape[1])).T[:, :1]


def iota(shape, dim):
    return lax.broadcasted_iota(jnp.int32, shape, dim)


def silu(x):
    return x / (1.0 + jnp.exp(-x))


def level_of(size):
    diff = jnp.bitwise_xor(iota((size, size), 0), iota((size, size), 1))
    level = jnp.zeros((size, size), jnp.int32)
    for bit in range(size.bit_length() - 1):
        level = level + (diff >= (1 << bit)).astype(jnp.int32)
    return level


def unit_lower_inverse(lower, level, eye):
    size = lower.shape[0]
    inverse = eye - jnp.where(level == 1, lower, 0.0)
    for step in range(2, size.bit_length()):
        joint = jnp.where(level == step, lower, 0.0)
        inverse = inverse - mm3(mm3(inverse, joint), inverse)
    return inverse


def recurrence(
    devices,
    repeat,
    pre_ref,
    gate_ref,
    taps_ref,
    logd_ref,
    beta_ref,
    seg_ref,
    gain_ref,
    out_ref,
    ext,
    tail,
    level_ref,
    gam_ref,
    local_out,
    edge,
    mmat,
    bmat,
    outgoing,
    incoming,
    tail_sems,
    send_sems,
    recv_sems,
):
    me = lax.axis_index("ctx")
    not_first = me > 0
    not_last = me < devices - 1
    barrier = pltpu.get_barrier_semaphore()

    @pl.when(not_first)
    def _():
        pl.semaphore_signal(barrier, inc=1, device_id={"ctx": me - 1}, device_id_type=MESH)

    @pl.when(not_last)
    def _():
        pl.semaphore_signal(barrier, inc=1, device_id={"ctx": me + 1}, device_id_type=MESH)

    pl.semaphore_wait(barrier, not_first.astype(jnp.int32) + not_last.astype(jnp.int32))

    count, width = pre_ref.shape
    heads_v = logd_ref.shape[0]
    heads_k = heads_v // repeat
    width_qk = heads_k * DK
    tail_copy = pltpu.make_async_remote_copy(
        src_ref=pre_ref.at[pl.ds(count - TAIL, TAIL)],
        dst_ref=tail,
        send_sem=tail_sems.at[0],
        recv_sem=tail_sems.at[1],
        device_id={"ctx": me + 1},
        device_id_type=MESH,
    )

    @pl.when(not_last)
    def _():
        tail_copy.start()

    level_ref[...] = level_of(HALF)
    upper = (iota((count, count), 0) <= iota((count, count), 1)).astype(F32)
    gam_ref[...] = lax.dot_general(
        logd_ref[...], upper, (((1,), (0,)), ((), ())), precision=lax.Precision.HIGHEST,
        preferred_element_type=F32,
    )
    ext[TAIL:, :] = pre_ref[...].astype(F32)

    @pl.when(jnp.logical_not(not_first))
    def _():
        ext[:TAIL, :] = jnp.zeros((TAIL, width), F32)

    @pl.when(not_first)
    def _():
        tail_copy.wait_recv()
        ext[:TAIL, :] = tail[...].astype(F32)

    offset = me * count
    seg_row = seg_ref[...].astype(F32)
    seg_col = column(seg_row)
    position = (offset + iota((count, 1), 0)).astype(F32)
    since = position - seg_col
    valids = [(since >= float(CONV - 1 - j)).astype(F32) for j in range(CONV)]
    enters = (seg_col < offset.astype(F32)).astype(F32)
    same_last = seg_col == jnp.max(seg_row, axis=1, keepdims=True)

    def conv(at):
        lanes = pl.ds(pl.multiple_of(at, 128), 128)
        total = None
        for j in range(CONV):
            term = ext[TAIL - (CONV - 1) + j : TAIL - (CONV - 1) + j + count, lanes] * (
                taps_ref[j : j + 1, lanes] * valids[j]
            )
            total = term if total is None else total + term
        return silu(total)

    def unit(x):
        return x * lax.rsqrt(jnp.sum(x * x, axis=-1, keepdims=True) + 1e-06)

    def per_key_head(kh, carry):
        query = unit(conv(kh * DK)) * DK ** (-0.5)
        key = unit(conv(width_qk + kh * DK))
        key_b = key.astype(BF16)
        keys_dot = mm(key_b, key_b, ((1,), (1,)))
        query_dot = mm(query.astype(BF16), key_b, ((1,), (1,)))
        rows, cols = iota((count, count), 0), iota((count, count), 1)
        same = seg_col == seg_row
        within = jnp.logical_and(rows >= cols, same)
        strict = jnp.logical_and(rows > cols, same)
        eye = (iota((HALF, HALF), 0) == iota((HALF, HALF), 1)).astype(F32)
        eye_s = eye
        level = level_ref[...]
        for sub in range(repeat):
            h = kh * repeat + sub
            value = conv(2 * width_qk + h * DV)
            gam_row = gam_ref[pl.ds(h, 1), :]
            gam_col = column(gam_row)
            beta_col = column(beta_ref[pl.ds(h, 1), :])
            decay = jnp.where(within, jnp.exp(jnp.where(within, gam_col - gam_row, 0.0)), 0.0)
            lead = jnp.exp(gam_col) * enters
            lower = jnp.where(strict, beta_col * keys_dot * decay, 0.0)
            rhs = jnp.concatenate([beta_col * value, (beta_col * lead) * key], axis=1)
            solved = []
            for b in range(count // HALF):
                r = slice(b * HALF, (b + 1) * HALF)
                inverse = unit_lower_inverse(lower[r, r], level, eye)
                part = rhs[r]
                if solved:
                    before = solved[0] if b == 1 else jnp.concatenate(solved, axis=0)
                    part = part - mm3(lower[r, : b * HALF], before)
                solved.append(mm3(inverse, part))
            w_both = jnp.concatenate(solved, axis=0)
            w_both_b = w_both.astype(BF16)
            mixed = mm((query_dot * decay).astype(BF16), w_both_b)
            lanes = pl.ds(pl.multiple_of(h * DV, 128), DV)
            local_out[:, lanes] = mixed[:, :DV]
            edge[:, lanes] = (lead * query - mixed[:, DV:]).astype(BF16)
            gam_last = gam_row[:, count - 1 :]
            last = jnp.where(same_last, jnp.exp(jnp.where(same_last, gam_last - gam_col, 0.0)), 0.0)
            maps = mm((w_both * last).astype(BF16), key_b, ((0,), (0,)))
            bmat[h] = maps[:DV]
            mmat[h] = lead[count - 1 :, :] * eye_s - maps[DV:]
        return carry

    lax.fori_loop(0, heads_k, per_key_head, 0)

    def chain(h, carry):
        copy = pltpu.make_async_remote_copy(
            src_ref=outgoing.at[h],
            dst_ref=incoming.at[h],
            send_sem=send_sems.at[h],
            recv_sem=recv_sems.at[h],
            device_id={"ctx": me + 1},
            device_id_type=MESH,
        )

        @pl.when(not_first)
        def _():
            copy.wait_recv()

        @pl.when(jnp.logical_not(not_first))
        def _():
            incoming[h] = jnp.zeros((DV, DK), BF16)

        state = incoming[h]

        @pl.when(not_last)
        def _():
            map_high, map_low = halves(mmat[h])
            outgoing[h] = (mm(state, map_high) + mm(state, map_low) + bmat[h]).astype(BF16)
            copy.start()

        lanes = pl.ds(pl.multiple_of(h * DV, 128), DV)
        recur = local_out[:, lanes] + mm(edge[:, lanes], state, ((1,), (1,)))
        scale = lax.rsqrt(jnp.mean(recur * recur, axis=-1, keepdims=True) + 1e-06)
        out_ref[:, lanes] = (recur * scale * gain_ref[...] * silu(gate_ref[:, lanes])).astype(BF16)
        return carry

    lax.fori_loop(0, heads_v, chain, 0)

    @pl.when(not_last)
    def _():
        tail_copy.wait_send()

        def drain(h, carry):
            pltpu.make_async_remote_copy(
                src_ref=outgoing.at[h],
                dst_ref=incoming.at[h],
                send_sem=send_sems.at[h],
                recv_sem=recv_sems.at[h],
                device_id={"ctx": me + 1},
                device_id_type=MESH,
            ).wait_send()
            return carry

        lax.fori_loop(0, heads_v, drain, 0)


def local(
    devices,
    tokens,
    w_query_key,
    w_value,
    w_gate_out,
    conv_query_key,
    conv_value,
    log_decay,
    beta,
    seg_start,
    norm_gain,
    w_output,
):
    width_qk = w_query_key.shape[2]
    width_v = w_value.shape[1]
    heads_k = width_qk // DK
    heads_v = width_v // DV
    count = seg_start.shape[0]
    width = 2 * width_qk + width_v
    piece = lax.all_gather(tokens, "tp", axis=0, tiled=True)
    pre = jnp.concatenate(
        [
            jnp.dot(piece, w_query_key[0], preferred_element_type=F32).astype(BF16),
            jnp.dot(piece, w_query_key[1], preferred_element_type=F32).astype(BF16),
            jnp.dot(piece, w_value, preferred_element_type=F32).astype(BF16),
        ],
        axis=1,
    )
    gate_lin = jnp.dot(piece, w_gate_out, preferred_element_type=F32)
    taps = jnp.concatenate([conv_query_key[0], conv_query_key[1], conv_value], axis=1)
    vmem = pl.BlockSpec(memory_space=pltpu.VMEM)
    normed = pl.pallas_call(
        functools.partial(recurrence, devices, heads_v // heads_k),
        out_shape=jax.ShapeDtypeStruct((count, width_v), BF16),
        in_specs=[vmem] * 7,
        out_specs=vmem,
        scratch_shapes=[
            pltpu.VMEM((TAIL + count, width), F32),
            pltpu.VMEM((TAIL, width), BF16),
            pltpu.VMEM((HALF, HALF), jnp.int32),
            pltpu.VMEM((heads_v, count), F32),
            pltpu.VMEM((count, width_v), F32),
            pltpu.VMEM((count, width_v), BF16),
            pltpu.VMEM((heads_v, DK, DK), F32),
            pltpu.VMEM((heads_v, DV, DK), F32),
            pltpu.VMEM((heads_v, DV, DK), BF16),
            pltpu.VMEM((heads_v, DV, DK), BF16),
            pltpu.SemaphoreType.DMA((2,)),
            pltpu.SemaphoreType.DMA((heads_v,)),
            pltpu.SemaphoreType.DMA((heads_v,)),
        ],
        compiler_params=pltpu.CompilerParams(
            collective_id=0, has_side_effects=True, vmem_limit_bytes=48 << 20
        ),
    )(pre, gate_lin, taps, log_decay, beta, seg_start.reshape(1, count), norm_gain.reshape(1, DV))
    return lax.psum_scatter(
        jnp.dot(normed, w_output, preferred_element_type=F32).astype(BF16),
        "tp",
        scatter_dimension=0,
        tiled=True,
    )


def solution(mesh):
    return jax.shard_map(
        functools.partial(local, mesh.shape["ctx"]),
        mesh=mesh,
        in_specs=(
            P(("ctx", "tp"), None),
            P(None, None, "tp"),
            P(None, "tp"),
            P(None, "tp"),
            P(None, None, "tp"),
            P(None, "tp"),
            P("tp", "ctx"),
            P("tp", "ctx"),
            P("ctx"),
            P(),
            P("tp", None),
        ),
        out_specs=P(("ctx", "tp"), None),
        check_vma=False,
    )
```

time: 420 us -> 136 us (0.32)
  other arithmetic: 167 us -> 0.83 us
  waiting for transfers between devices: 122 us -> 44.8 us
  matrix products: 82.1 us -> 11.1 us
  Pallas kernels: 0 us -> 62.6 us
  starting transfers between devices: 17.3 us -> 0.04 us
  local copies, waits for them, and re-layouts: 14.4 us -> 1.15 us
    another operation x5 -> x0, other arithmetic: 160 us -> none  [the longest x4 159 us: stretch_parts(): lax.linalg.triangular_solve(lower_mat, (betas * lead)[:, :, None] * key,...]
    ppermute x8 -> x0, waiting for transfers between devices: 83.5 us -> none  [passed_along(): return lax.ppermute(array, axis, pairs)]
    dot_general x33 -> x5, matrix products: 77.9 us -> 11.1 us  [the longest x1 2.76 us: local(): jnp.dot(piece, w_query_key[0], preferred_element_type=F32).astype(BF16)]
    pallas_call x0 -> x1, Pallas kernels: none -> 62.6 us  [local(): pl.pallas_call(functools.partial(recurrence, devices, heads_v // heads_k)...]
    ppermute x8 -> x0, starting transfers between devices: 17.3 us -> none  [passed_along(): return lax.ppermute(array, axis, pairs)]
    unnamed x15 -> x18, local copies, waits for them, and re-layouts: 6.28 us -> 0.43 us
    all_gather x1, waiting for transfers between devices: 13.3 us -> 17.9 us  [local(): piece = lax.all_gather(tokens, 'tp', axis=0, tiled=True)]
    another operation x2 -> x0, matrix products: 4.21 us -> none  [the longest x1 2.11 us: stretch_parts(): lax.linalg.triangular_solve(lower_mat, (betas * lead)[:, :, None] * key,...]
  transfers between devices with their start and end apart: 10 -> 2, of which waited for: 10 -> 2; matrix products, arithmetic and copies ran while one was open for 2% -> 1% of each run, Pallas kernels for 0% -> 0%
where the time goes in v1:
time: 136 us; the launch traced here: 134 us
  Pallas kernels  62.6 us (46%)
  waiting for transfers between devices  44.8 us (33%)
  between operations  13.5 us (10%)
  matrix products  11.1 us (8%)
    pallas_call x1, Pallas kernels, local(): pl.pallas_call(functools.partial(recurrence, devices, heads_v // heads_k)...  62.6 us
    reduce_scatter x1, waiting for transfers between devices, local(): lax.psum_scatter(jnp.dot(normed, w_output, preferred_element_type=F32).as...  26.2 us
    all_gather x1, waiting for transfers between devices, local(): piece = lax.all_gather(tokens, 'tp', axis=0, tiled=True)  17.9 us
    dot_general x1, matrix products, local(): jnp.dot(piece, w_query_key[0], preferred_element_type=F32).astype(BF16)  2.76 us
  transfers between devices with their start and end apart: 2, of which 2 were waited for; matrix products, arithmetic and copies ran while one was open for 1% of the time, Pallas kernels for 0%

profile of v1, /device:TPU:24, one launch (start us, length us, event | category | flops | bytes accessed | tf_op | source)
XLA Modules:
  0.0 134.0 jit_solution(7936224236398127276)
XLA Ops:
  6.5 0.0 all-gather.2.cloned.1.call-start
  6.5 0.7 all-gather.2.cloned.1.call-update
  7.3 0.0 reduce-scatter.2.cloned.1.call-start
  7.3 0.7 slice_bitcast_fusion.1
  8.0 0.7 pad_maximum_fusion.1.taps_ref
  8.7 17.9 %all-gather.2.cloned.1.call-done = bf16[256,2048]{1,0:T(8,128)(2,1)} async-done(((bf16[64,2048]{1,0:T(8,128)(2,1)}), bf16[256,2048]{1,0:T(8,128)(2,1)}) %all-gather.2.cloned.1.call-update) | async-done | bytes 1048592 | tf_op jit(solution)/shard_map/all_gather | solution.py:280
  26.7 0.0 copy-start.4
  26.7 0.0 copy-start.5
  26.7 2.8 %fusion.6 = bf16[256,512]{1,0:T(8,128)(2,1)S(1)} fusion(bf16[256,2048]{1,0:T(8,128)(2,1)} %all-gather.2.cloned.1.call-done, bf16[2,2048,512]{2,1,0:T(8,128)(2,1)} %param.12), kind=kOutput, calls=%fused_computation.8 | convolution fusion | flops 537001984 | bytes 3407872 | tf_op jit(solution)/shard_map/dot_general | solution.py:283
  29.4 0.4 copy-done.4
  29.8 2.2 %fusion.9 = bf16[256,512]{1,0:T(8,128)(2,1)S(1)} fusion(bf16[256,2048]{1,0:T(8,128)(2,1)} %all-gather.2.cloned.1.call-done, bf16[2,2048,512]{2,1,0:T(8,128)(2,1)S(1)} %copy-done.4), kind=kOutput, calls=%fused_computation.9 | convolution fusion | flops 537001984 | bytes 3407872 | tf_op jit(solution)/shard_map/dot_general | solution.py:284
  32.0 0.0 copy-done.5
  32.0 0.0 copy-start.6
  32.0 0.0 copy-start.8
  32.0 2.6 %convolution_convert_fusion.1 = bf16[256,1024]{1,0:T(8,128)(2,1)S(1)} fusion(bf16[256,2048]{1,0:T(8,128)(2,1)} %all-gather.2.cloned.1.call-done, bf16[2048,1024]{1,0:T(8,128)(2,1)S(1)} %copy-done.5), kind=kOutput, calls=%fused_computation.7 | convolution fusion | flops 1074003968 | bytes 5767168 | tf_op jit(solution)/shard_map/dot_general | solution.py:285
  34.6 0.1 pad_maximum_fusion.pre_ref
  34.8 0.0 copy-done.6
  34.8 0.0 copy-done.8
  34.8 0.0 copy-start
  34.8 0.0 copy-start.1
  34.8 0.0 copy-start.2
  34.8 0.0 copy-start.3
  34.8 0.0 copy-start.7
  34.8 1.3 fusion.12.gate_ref
  36.1 0.0 copy-done
  36.2 0.0 copy-done.1
  36.2 0.0 copy-done.2
  36.2 0.0 copy-done.3
  36.2 62.6 %shard_map.109 = bf16[256,1024]{1,0:T(8,128)(2,1)S(1)} custom-call(bf16[256,2048]{1,0:T(8,128)(2,1)S(1)} %pad_maximum_fusion.pre_ref, f32[256,1024]{1,0:T(8,128)S(1)} %fusion.12.gate_ref, f32[4,2048]{1,0:T(4,128)S(1)} %pad_maximum_fusion.1.taps_ref, f32[8,256]{1,0:T(8,128)S(1)} %copy-done, f32[8,256]{1,0:T(8,128)S(1)} %copy-done.1, s32[1,256]{1,0:T(1,128)S(1)} %bitcast.24, ...), custom_call_target="tpu_custom_call" | custom-call | tf_op jit(solution)/shard_map/pallas_call | solution.py:292
  98.8 0.0 copy-done.7
  98.8 2.2 %convolution_convert_fusion = bf16[256,2048]{1,0:T(8,128)(2,1)} fusion(bf16[256,1024]{1,0:T(8,128)(2,1)S(1)} %shard_map.109, bf16[1024,2048]{1,0:T(8,128)(2,1)S(1)} %copy-done.7), kind=kOutput, calls=%fused_computation | convolution fusion | flops 1074266112 | bytes 5767168 | tf_op jit(solution)/shard_map/dot_general | solution.py:317
  101.0 0.0 reduce-scatter.2.cloned.1.call-update
  101.0 26.2 %reduce-scatter.2.cloned.1.call-done = bf16[64,2048]{1,0:T(8,128)(2,1)} async-done(((bf16[256,2048]{1,0:T(8,128)(2,1)}), bf16[64,2048]{1,0:T(8,128)(2,1)}) %reduce-scatter.2.cloned.1.call-update) | async-done | bytes 262160 | tf_op jit(solution)/shard_map/reduce_scatter | solution.py:316
Async XLA Ops:
  6.5 20.1 %all-gather.2.cloned.1.call-start = ((), (), s32[]{:S(2)}) async-start(), calls=%async_computation.1 | async-start | bytes 1310720 | tf_op jit(solution)/shard_map/all_gather | solution.py:280
  7.3 119.9 %reduce-scatter.2.cloned.1.call-start = ((), (), s32[]{:S(2)}) async-start(), calls=%async_computation.2 | async-start | bytes 1310720 | tf_op jit(solution)/shard_map/reduce_scatter | solution.py:316
  26.7 3.1 %copy-start.4 = (bf16[2,2048,512]{2,1,0:T(8,128)(2,1)S(1)}, bf16[2,2048,512]{2,1,0:T(8,128)(2,1)}, u32[]{:S(2)}) copy-start(bf16[2,2048,512]{2,1,0:T(8,128)(2,1)} %param.12) | copy-start | bytes 12582916
  26.7 5.3 %copy-start.5 = (bf16[2048,1024]{1,0:T(8,128)(2,1)S(1)}, bf16[2048,1024]{1,0:T(8,128)(2,1)}, u32[]{:S(2)}) copy-start(bf16[2048,1024]{1,0:T(8,128)(2,1)} %param.13) | copy-start | bytes 12582916
  32.0 2.8 %copy-start.6 = (bf16[2048,1024]{1,0:T(8,128)(2,1)S(1)}, bf16[2048,1024]{1,0:T(8,128)(2,1)}, u32[]{:S(2)}) copy-start(bf16[2048,1024]{1,0:T(8,128)(2,1)} %param.14) | copy-start | bytes 12582916
  32.0 2.8 %copy-start.8 = (bf16[256,2048]{1,0:T(8,128)(2,1)S(1)}, bf16[256,2048]{1,0:T(8,128)(2,1)}, u32[]{:S(2)}) copy-start(bf16[256,2048]{1,0:T(8,128)(2,1)} %all-gather.2.cloned.1.call-done) | copy-start | bytes 3145732
  34.8 1.3 %copy-start = (f32[8,256]{1,0:T(8,128)S(1)}, f32[8,256]{1,0:T(8,128)}, u32[]{:S(2)}) copy-start(f32[8,256]{1,0:T(8,128)} %logd_ref.1) | copy-start | bytes 24580
  34.8 1.4 %copy-start.1 = (f32[8,256]{1,0:T(8,128)S(1)}, f32[8,256]{1,0:T(8,128)}, u32[]{:S(2)}) copy-start(f32[8,256]{1,0:T(8,128)} %beta_ref.1) | copy-start | bytes 24580
  34.8 1.4 %copy-start.2 = (s32[256]{0:T(256)S(1)}, s32[256]{0:T(256)}, u32[]{:S(2)}) copy-start(s32[256]{0:T(256)} %param.19) | copy-start | bytes 3076
  34.8 1.4 %copy-start.3 = (f32[128]{0:T(128)S(1)}, f32[128]{0:T(128)}, u32[]{:S(2)}) copy-start(f32[128]{0:T(128)} %param.20) | copy-start | bytes 1540
  34.8 63.9 %copy-start.7 = (bf16[1024,2048]{1,0:T(8,128)(2,1)S(1)}, bf16[1024,2048]{1,0:T(8,128)(2,1)}, u32[]{:S(2)}) copy-start(bf16[1024,2048]{1,0:T(8,128)(2,1)} %param.21) | copy-start | bytes 12582916
Sparse Core Ops, SparseCore 0:
  8.9 17.6 all-gather.1
  101.1 25.9 reduce-scatter.1

commit v2 on v1

--- a/solution.py
+++ b/solution.py
@@ -12,6 +12,8 @@
 CONV = 4
 TAIL = 16
 HALF = 128
+TILE = 256
+OUT_TILE = 512
 
 MESH = pl.DeviceIdType.MESH
 F32 = jnp.float32
@@ -62,17 +64,29 @@
     return inverse
 
 
-def recurrence(
+def layer(
     devices,
+    peers,
     repeat,
-    pre_ref,
-    gate_ref,
+    tokens_ref,
     taps_ref,
     logd_ref,
     beta_ref,
     seg_ref,
     gain_ref,
+    w_query_key_hbm,
+    w_value_hbm,
+    w_gate_hbm,
+    w_output_hbm,
     out_ref,
+    w_query_key,
+    w_value,
+    w_gate,
+    w_output,
+    gathered,
+    tail_out,
+    gate_ref,
+    normed,
     ext,
     tail,
     level_ref,
@@ -83,13 +97,58 @@
     bmat,
     outgoing,
     incoming,
+    core_out,
+    core_in,
+    chip_out,
+    chip_in,
+    total,
+    weight_sems,
     tail_sems,
     send_sems,
     recv_sems,
+    gather_send,
+    gather_recv,
+    pass_send,
+    pass_recv,
+    core_send,
+    core_recv,
+    chip_send,
+    chip_recv,
 ):
     me = lax.axis_index("ctx")
+    slot = lax.axis_index("tp")
+    core, chip, chips = slot % 2, slot // 2, peers // 2
+    partner = chip * 2 + 1 - core
     not_first = me > 0
     not_last = me < devices - 1
+    rows, depth = tokens_ref.shape
+    count = rows * peers
+    heads_v = logd_ref.shape[0]
+    heads_k = heads_v // repeat
+    width_qk = heads_k * DK
+    width_v = heads_v * DV
+    width = 2 * width_qk + width_v
+
+    loads = [
+        pltpu.make_async_copy(src, dst, weight_sems.at[n])
+        for n, (src, dst) in enumerate(
+            [
+                (w_query_key_hbm, w_query_key),
+                (w_value_hbm, w_value),
+                (w_gate_hbm, w_gate),
+                (w_output_hbm, w_output),
+            ]
+        )
+    ]
+    for load in loads:
+        load.start()
+
+    def chip_at(d):
+        return lax.rem(chip + d, chips)
+
+    def on_chip(d):
+        return {"tp": chip_at(d) * 2 + core}
+
     barrier = pltpu.get_barrier_semaphore()
 
     @pl.when(not_first)
@@ -100,24 +159,28 @@
     def _():
         pl.semaphore_signal(barrier, inc=1, device_id={"ctx": me + 1}, device_id_type=MESH)
 
-    pl.semaphore_wait(barrier, not_first.astype(jnp.int32) + not_last.astype(jnp.int32))
-
-    count, width = pre_ref.shape
-    heads_v = logd_ref.shape[0]
-    heads_k = heads_v // repeat
-    width_qk = heads_k * DK
-    tail_copy = pltpu.make_async_remote_copy(
-        src_ref=pre_ref.at[pl.ds(count - TAIL, TAIL)],
-        dst_ref=tail,
-        send_sem=tail_sems.at[0],
-        recv_sem=tail_sems.at[1],
-        device_id={"ctx": me + 1},
-        device_id_type=MESH,
-    )
-
-    @pl.when(not_last)
-    def _():
-        tail_copy.start()
+    pl.semaphore_signal(barrier, inc=1, device_id={"tp": partner}, device_id_type=MESH)
+    for d in range(1, chips):
+        pl.semaphore_signal(barrier, inc=1, device_id=on_chip(d), device_id_type=MESH)
+    pl.semaphore_wait(barrier, not_first.astype(jnp.int32) + not_last.astype(jnp.int32) + chips)
+
+    def remote(src, dst, send, recv, device):
+        return pltpu.make_async_remote_copy(
+            src_ref=src, dst_ref=dst, send_sem=send, recv_sem=recv, device_id=device, device_id_type=MESH
+        )
+
+    def block(index):
+        return gathered.at[pl.ds(pl.multiple_of(index * rows, 16), rows)]
+
+    across = [
+        remote(tokens_ref, block(slot), gather_send.at[d], gather_recv.at[d], on_chip(d))
+        for d in range(1, chips)
+    ]
+    for copy in across:
+        copy.start()
+    passes = [remote(tokens_ref, block(slot), pass_send.at[0], pass_recv.at[0], {"tp": partner})]
+    passes[0].start()
+    gathered[pl.ds(pl.multiple_of(slot * rows, 16), rows), :] = tokens_ref[...]
 
     level_ref[...] = level_of(HALF)
     upper = (iota((count, count), 0) <= iota((count, count), 1)).astype(F32)
@@ -125,7 +188,46 @@
         logd_ref[...], upper, (((1,), (0,)), ((), ())), precision=lax.Precision.HIGHEST,
         preferred_element_type=F32,
     )
-    ext[TAIL:, :] = pre_ref[...].astype(F32)
+
+    for d in range(1, chips):
+        across[d - 1].wait_recv()
+        came = chip_at(chips - d) * 2 + core
+        passes.append(remote(block(came), block(came), pass_send.at[d], pass_recv.at[d], {"tp": partner}))
+        passes[d].start()
+    for copy in passes:
+        copy.wait_recv()
+
+    def project_pre(weight, first, columns):
+        def tile(t, carry):
+            lanes = pl.ds(pl.multiple_of(t * TILE, TILE), TILE)
+            to = pl.ds(pl.multiple_of(first + t * TILE, TILE), TILE)
+            part = mm(gathered[...], weight[:, lanes]).astype(BF16)
+            ext[TAIL:, to] = part.astype(F32)
+            tail_out[:, to] = part[count - TAIL :]
+            return carry
+
+        lax.fori_loop(0, columns // TILE, tile, 0)
+
+    loads[0].wait()
+    project_pre(w_query_key.at[0], 0, width_qk)
+    project_pre(w_query_key.at[1], width_qk, width_qk)
+    loads[1].wait()
+    project_pre(w_value, 2 * width_qk, width_v)
+
+    tail_copy = remote(tail_out, tail, tail_sems.at[0], tail_sems.at[1], {"ctx": me + 1})
+
+    @pl.when(not_last)
+    def _():
+        tail_copy.start()
+
+    loads[2].wait()
+
+    def project_gate(t, carry):
+        lanes = pl.ds(pl.multiple_of(t * TILE, TILE), TILE)
+        gate_ref[:, lanes] = mm(gathered[...], w_gate[:, lanes])
+        return carry
+
+    lax.fori_loop(0, width_v // TILE, project_gate, 0)
 
     @pl.when(jnp.logical_not(not_first))
     def _():
@@ -234,10 +336,73 @@
         lanes = pl.ds(pl.multiple_of(h * DV, 128), DV)
         recur = local_out[:, lanes] + mm(edge[:, lanes], state, ((1,), (1,)))
         scale = lax.rsqrt(jnp.mean(recur * recur, axis=-1, keepdims=True) + 1e-06)
-        out_ref[:, lanes] = (recur * scale * gain_ref[...] * silu(gate_ref[:, lanes])).astype(BF16)
+        normed[:, lanes] = (recur * scale * gain_ref[...] * silu(gate_ref[:, lanes])).astype(BF16)
         return carry
 
     lax.fori_loop(0, heads_v, chain, 0)
+
+    loads[3].wait()
+    tiles = depth // OUT_TILE
+
+    def rows_for(which):
+        return jnp.concatenate(
+            [
+                normed[pl.ds(pl.multiple_of((chip_at(d) * 2 + which) * rows, 16), rows), :]
+                for d in range(chips)
+            ],
+            axis=0,
+        )
+
+    def core_copy(t):
+        return remote(core_out.at[t], core_in.at[t], core_send.at[t], core_recv.at[t], {"tp": partner})
+
+    def chip_copy(t, d):
+        return remote(
+            chip_out.at[t, d - 1], chip_in.at[t, d - 1], chip_send.at[t, d - 1], chip_recv.at[t, d - 1], on_chip(d)
+        )
+
+    def for_partner(t, carry):
+        lanes = pl.ds(pl.multiple_of(t * OUT_TILE, OUT_TILE), OUT_TILE)
+        core_out[t] = mm(rows_for(1 - core), w_output[:, lanes]).astype(BF16)
+        core_copy(t).start()
+        return carry
+
+    lax.fori_loop(0, tiles, for_partner, 0)
+
+    def for_core(t, carry):
+        lanes = pl.ds(pl.multiple_of(t * OUT_TILE, OUT_TILE), OUT_TILE)
+        part = mm(rows_for(core), w_output[:, lanes])
+        core_copy(t).wait_recv()
+        part = part + core_in[t].astype(F32)
+        for d in range(1, chips):
+            chip_out[t, d - 1] = part[d * rows : (d + 1) * rows].astype(BF16)
+            chip_copy(t, d).start()
+        total[:, lanes] = part[:rows]
+        return carry
+
+    lax.fori_loop(0, tiles, for_core, 0)
+
+    def finish(t, carry):
+        lanes = pl.ds(pl.multiple_of(t * OUT_TILE, OUT_TILE), OUT_TILE)
+        part = total[:, lanes]
+        for d in range(1, chips):
+            chip_copy(t, d).wait_recv()
+            part = part + chip_in[t, d - 1].astype(F32)
+        out_ref[:, lanes] = part.astype(BF16)
+        return carry
+
+    lax.fori_loop(0, tiles, finish, 0)
+
+    for copy in across + passes:
+        copy.wait_send()
+
+    def drain_sums(t, carry):
+        core_copy(t).wait_send()
+        for d in range(1, chips):
+            chip_copy(t, d).wait_send()
+        return carry
+
+    lax.fori_loop(0, tiles, drain_sums, 0)
 
     @pl.when(not_last)
     def _():
@@ -259,6 +424,7 @@
 
 def local(
     devices,
+    peers,
     tokens,
     w_query_key,
     w_value,
@@ -276,25 +442,29 @@
     heads_k = width_qk // DK
     heads_v = width_v // DV
     count = seg_start.shape[0]
+    rows, depth = tokens.shape
     width = 2 * width_qk + width_v
-    piece = lax.all_gather(tokens, "tp", axis=0, tiled=True)
-    pre = jnp.concatenate(
-        [
-            jnp.dot(piece, w_query_key[0], preferred_element_type=F32).astype(BF16),
-            jnp.dot(piece, w_query_key[1], preferred_element_type=F32).astype(BF16),
-            jnp.dot(piece, w_value, preferred_element_type=F32).astype(BF16),
-        ],
-        axis=1,
-    )
-    gate_lin = jnp.dot(piece, w_gate_out, preferred_element_type=F32)
+    chips = peers // 2
+    others = max(chips - 1, 1)
+    tiles = depth // OUT_TILE
     taps = jnp.concatenate([conv_query_key[0], conv_query_key[1], conv_value], axis=1)
     vmem = pl.BlockSpec(memory_space=pltpu.VMEM)
-    normed = pl.pallas_call(
-        functools.partial(recurrence, devices, heads_v // heads_k),
-        out_shape=jax.ShapeDtypeStruct((count, width_v), BF16),
-        in_specs=[vmem] * 7,
+    anywhere = pl.BlockSpec(memory_space=pl.ANY)
+    dma = pltpu.SemaphoreType.DMA
+    return pl.pallas_call(
+        functools.partial(layer, devices, peers, heads_v // heads_k),
+        out_shape=jax.ShapeDtypeStruct((rows, depth), BF16),
+        in_specs=[vmem] * 6 + [anywhere] * 4,
         out_specs=vmem,
         scratch_shapes=[
+            pltpu.VMEM(w_query_key.shape, BF16),
+            pltpu.VMEM(w_value.shape, BF16),
+            pltpu.VMEM(w_gate_out.shape, BF16),
+            pltpu.VMEM(w_output.shape, BF16),
+            pltpu.VMEM((count, depth), BF16),
+            pltpu.VMEM((TAIL, width), BF16),
+            pltpu.VMEM((count, width_v), F32),
+            pltpu.VMEM((count, width_v), BF16),
             pltpu.VMEM((TAIL + count, width), F32),
             pltpu.VMEM((TAIL, width), BF16),
             pltpu.VMEM((HALF, HALF), jnp.int32),
@@ -305,25 +475,44 @@
             pltpu.VMEM((heads_v, DV, DK), F32),
             pltpu.VMEM((heads_v, DV, DK), BF16),
             pltpu.VMEM((heads_v, DV, DK), BF16),
-            pltpu.SemaphoreType.DMA((2,)),
-            pltpu.SemaphoreType.DMA((heads_v,)),
-            pltpu.SemaphoreType.DMA((heads_v,)),
+            pltpu.VMEM((tiles, chips * rows, OUT_TILE), BF16),
+            pltpu.VMEM((tiles, chips * rows, OUT_TILE), BF16),
+            pltpu.VMEM((tiles, others, rows, OUT_TILE), BF16),
+            pltpu.VMEM((tiles, others, rows, OUT_TILE), BF16),
+            pltpu.VMEM((rows, depth), F32),
+            dma((4,)),
+            dma((2,)),
+            dma((heads_v,)),
+            dma((heads_v,)),
+            dma((chips,)),
+            dma((chips,)),
+            dma((chips,)),
+            dma((chips,)),
+            dma((tiles,)),
+            dma((tiles,)),
+            dma((tiles, others)),
+            dma((tiles, others)),
         ],
         compiler_params=pltpu.CompilerParams(
-            collective_id=0, has_side_effects=True, vmem_limit_bytes=48 << 20
+            collective_id=0, has_side_effects=True, vmem_limit_bytes=56 << 20
         ),
-    )(pre, gate_lin, taps, log_decay, beta, seg_start.reshape(1, count), norm_gain.reshape(1, DV))
-    return lax.psum_scatter(
-        jnp.dot(normed, w_output, preferred_element_type=F32).astype(BF16),
-        "tp",
-        scatter_dimension=0,
-        tiled=True,
+    )(
+        tokens,
+        taps,
+        log_decay,
+        beta,
+        seg_start.reshape(1, count),
+        norm_gain.reshape(1, DV),
+        w_query_key,
+        w_value,
+        w_gate_out,
+        w_output,
     )
 
 
 def solution(mesh):
     return jax.shard_map(
-        functools.partial(local, mesh.shape["ctx"]),
+        functools.partial(local, mesh.shape["ctx"], mesh.shape["tp"]),
         mesh=mesh,
         in_specs=(
             P(("ctx", "tp"), None),

time: 136 us -> 91.9 us (0.68)
  the two profiles are of different devices: /device:TPU:24 before, /device:TPU:26 now
where the time goes in v2:
time: 91.9 us; the launch traced here: 91.5 us
  Pallas kernels  87.8 us (96%)
  local copies, waits for them, and re-layouts  2.39 us (3%)
  other arithmetic  1.34 us (1%)
    pallas_call x1, Pallas kernels, local(): pl.pallas_call(functools.partial(layer, devices, peers, heads_v // heads_...  87.8 us

profile of v2, /device:TPU:26, one launch (start us, length us, event | category | flops | bytes accessed | tf_op | source)
XLA Modules:
  0.0 91.5 jit_solution(2847065987317151108)
XLA Ops:
  0.0 0.7 slice_bitcast_fusion.1
  0.7 1.3 %pad_maximum_fusion.taps_ref = f32[4,2048]{1,0:T(4,128)} fusion(f32[4,1024]{1,0:T(4,128)} %param.16, f32[4,512]{1,0:T(4,128)S(1)} %get-tuple-element.6, f32[4,512]{1,0:T(4,128)S(1)} %get-tuple-element.5), kind=kLoop, calls=%fused_computation | loop fusion | flops 16384 | bytes 65536 | tf_op jit(solution)/shard_map/concatenate | solution.py:450
  2.1 87.8 %shard_map.109 = bf16[64,2048]{1,0:T(8,128)(2,1)} custom-call(bf16[64,2048]{1,0:T(8,128)(2,1)} %tokens_ref.1, f32[4,2048]{1,0:T(4,128)} %pad_maximum_fusion.taps_ref, f32[8,256]{1,0:T(8,128)} %logd_ref.1, f32[8,256]{1,0:T(8,128)} %beta_ref.1, s32[1,256]{1,0:T(1,128)} %bitcast.6, f32[1,128]{1,0:T(1,128)} %bitcast.7, bf16[2,2048,512]{2,1,0:T(8,128)(2,1)} %w_query_key_hbm.1, ...), custom_call_target="tpu_custom_call" | custom-call | tf_op jit(solution)/shard_map/pallas_call | solution.py:454
  89.9 1.7 %copy.13 = bf16[64,2048]{1,0:T(8,128)(2,1)} copy(bf16[64,2048]{1,0:T(8,128)(2,1)} %shard_map.109) | data formatting | bytes 524288

commit v3 on v2

--- a/solution.py
+++ b/solution.py
@@ -55,13 +55,17 @@
     return level
 
 
-def unit_lower_inverse(lower, level, eye):
-    size = lower.shape[0]
-    inverse = eye - jnp.where(level == 1, lower, 0.0)
+def unit_lower_inverses(lowers, level, eye):
+    size = lowers[0].shape[0]
+    inverses = [eye - jnp.where(level == 1, lower, 0.0) for lower in lowers]
     for step in range(2, size.bit_length()):
-        joint = jnp.where(level == step, lower, 0.0)
-        inverse = inverse - mm3(mm3(inverse, joint), inverse)
-    return inverse
+        joints = [jnp.where(level == step, lower, 0.0).astype(BF16) for lower in lowers]
+        rounded = [inverse.astype(BF16) for inverse in inverses]
+        firsts = [mm(x, joint).astype(BF16) for x, joint in zip(rounded, joints)]
+        seconds = [mm(first, x) for first, x in zip(firsts, rounded)]
+        inverses = [inverse - second for inverse, second in zip(inverses, seconds)]
+    rests = [eye - inverse - mm3(lower, inverse) for lower, inverse in zip(lowers, inverses)]
+    return [inverse + mm(inverse.astype(BF16), rest.astype(BF16)) for inverse, rest in zip(inverses, rests)]
 
 
 def layer(
@@ -69,7 +73,8 @@
     peers,
     repeat,
     tokens_ref,
-    taps_ref,
+    taps_query_key,
+    taps_value,
     logd_ref,
     beta_ref,
     seg_ref,
@@ -91,9 +96,11 @@
     tail,
     level_ref,
     gam_ref,
-    local_out,
-    edge,
-    mmat,
+    keys,
+    decays,
+    corrected,
+    map_high,
+    map_low,
     bmat,
     outgoing,
     incoming,
@@ -247,12 +254,13 @@
     enters = (seg_col < offset.astype(F32)).astype(F32)
     same_last = seg_col == jnp.max(seg_row, axis=1, keepdims=True)
 
-    def conv(at):
+    def conv(at, taps_ref, tap_at):
         lanes = pl.ds(pl.multiple_of(at, 128), 128)
+        tap_lanes = pl.ds(pl.multiple_of(tap_at, 128), 128)
         total = None
         for j in range(CONV):
             term = ext[TAIL - (CONV - 1) + j : TAIL - (CONV - 1) + j + count, lanes] * (
-                taps_ref[j : j + 1, lanes] * valids[j]
+                taps_ref[j : j + 1, tap_lanes] * valids[j]
             )
             total = term if total is None else total + term
         return silu(total)
@@ -260,86 +268,106 @@
     def unit(x):
         return x * lax.rsqrt(jnp.sum(x * x, axis=-1, keepdims=True) + 1e-06)
 
-    def per_key_head(kh, carry):
-        query = unit(conv(kh * DK)) * DK ** (-0.5)
-        key = unit(conv(width_qk + kh * DK))
+    def state_copy(g):
+        return remote(outgoing.at[g], incoming.at[g], send_sems.at[g], recv_sems.at[g], {"ctx": me + 1})
+
+    def head_lanes(h):
+        return pl.ds(pl.multiple_of(h * DV, 128), DV)
+
+    def pass_state(g):
+        @pl.when(not_first)
+        def _():
+            state_copy(g).wait_recv()
+
+        @pl.when(jnp.logical_not(not_first))
+        def _():
+            incoming[g] = jnp.zeros((repeat * DV, DK), BF16)
+
+        @pl.when(not_last)
+        def _():
+            for sub in range(repeat):
+                h = g * repeat + sub
+                part = slice(sub * DV, (sub + 1) * DV)
+                state = incoming[g, part, :]
+                outgoing[g, part, :] = (mm(state, map_high[h]) + mm(state, map_low[h]) + bmat[h]).astype(BF16)
+            state_copy(g).start()
+
+    ahead = jnp.minimum(me, heads_k)
+    eye = (iota((HALF, HALF), 0) == iota((HALF, HALF), 1)).astype(F32)
+    parts = [slice(b * HALF, (b + 1) * HALF) for b in range(count // HALF)]
+
+    def key_side(g, carry):
+        key = unit(conv(width_qk + g * DK, taps_query_key.at[1], g * DK))
         key_b = key.astype(BF16)
+        keys[:, head_lanes(g)] = key_b
         keys_dot = mm(key_b, key_b, ((1,), (1,)))
-        query_dot = mm(query.astype(BF16), key_b, ((1,), (1,)))
-        rows, cols = iota((count, count), 0), iota((count, count), 1)
-        same = seg_col == seg_row
-        within = jnp.logical_and(rows >= cols, same)
-        strict = jnp.logical_and(rows > cols, same)
-        eye = (iota((HALF, HALF), 0) == iota((HALF, HALF), 1)).astype(F32)
-        eye_s = eye
+        rows_i, cols_i = iota((count, count), 0), iota((count, count), 1)
+        within = jnp.logical_and(rows_i >= cols_i, seg_col == seg_row)
+        strict = jnp.logical_and(rows_i > cols_i, within)
         level = level_ref[...]
+        lowers, sides, lasts, leads = [], [], [], []
         for sub in range(repeat):
-            h = kh * repeat + sub
-            value = conv(2 * width_qk + h * DV)
+            h = g * repeat + sub
+            value = conv(2 * width_qk + h * DV, taps_value, h * DV)
             gam_row = gam_ref[pl.ds(h, 1), :]
             gam_col = column(gam_row)
             beta_col = column(beta_ref[pl.ds(h, 1), :])
             decay = jnp.where(within, jnp.exp(jnp.where(within, gam_col - gam_row, 0.0)), 0.0)
+            decays[h] = decay
             lead = jnp.exp(gam_col) * enters
-            lower = jnp.where(strict, beta_col * keys_dot * decay, 0.0)
-            rhs = jnp.concatenate([beta_col * value, (beta_col * lead) * key], axis=1)
-            solved = []
-            for b in range(count // HALF):
-                r = slice(b * HALF, (b + 1) * HALF)
-                inverse = unit_lower_inverse(lower[r, r], level, eye)
-                part = rhs[r]
-                if solved:
-                    before = solved[0] if b == 1 else jnp.concatenate(solved, axis=0)
-                    part = part - mm3(lower[r, : b * HALF], before)
-                solved.append(mm3(inverse, part))
-            w_both = jnp.concatenate(solved, axis=0)
-            w_both_b = w_both.astype(BF16)
-            mixed = mm((query_dot * decay).astype(BF16), w_both_b)
-            lanes = pl.ds(pl.multiple_of(h * DV, 128), DV)
-            local_out[:, lanes] = mixed[:, :DV]
-            edge[:, lanes] = (lead * query - mixed[:, DV:]).astype(BF16)
+            lowers.append(jnp.where(strict, beta_col * keys_dot * decay, 0.0))
+            sides.append(jnp.concatenate([beta_col * value, (beta_col * lead) * key], axis=1))
             gam_last = gam_row[:, count - 1 :]
-            last = jnp.where(same_last, jnp.exp(jnp.where(same_last, gam_last - gam_col, 0.0)), 0.0)
-            maps = mm((w_both * last).astype(BF16), key_b, ((0,), (0,)))
+            lasts.append(jnp.where(same_last, jnp.exp(jnp.where(same_last, gam_last - gam_col, 0.0)), 0.0))
+            leads.append(lead[count - 1 :, :])
+        inverses = unit_lower_inverses([lower[r, r] for lower in lowers for r in parts], level, eye)
+        solved = [[] for _ in range(repeat)]
+        for b, r in enumerate(parts):
+            for sub in range(repeat):
+                part = sides[sub][r]
+                if b:
+                    part = part - mm3(lowers[sub][r, : b * HALF], jnp.concatenate(solved[sub], axis=0))
+                solved[sub].append(mm3(inverses[sub * len(parts) + b], part))
+        for sub in range(repeat):
+            h = g * repeat + sub
+            w_both = jnp.concatenate(solved[sub], axis=0)
+            corrected[h] = w_both.astype(BF16)
+            maps = mm((w_both * lasts[sub]).astype(BF16), key_b, ((0,), (0,)))
             bmat[h] = maps[:DV]
-            mmat[h] = lead[count - 1 :, :] * eye_s - maps[DV:]
-        return carry
-
-    lax.fori_loop(0, heads_k, per_key_head, 0)
-
-    def chain(h, carry):
-        copy = pltpu.make_async_remote_copy(
-            src_ref=outgoing.at[h],
-            dst_ref=incoming.at[h],
-            send_sem=send_sems.at[h],
-            recv_sem=recv_sems.at[h],
-            device_id={"ctx": me + 1},
-            device_id_type=MESH,
-        )
-
-        @pl.when(not_first)
+            map_high[h], map_low[h] = halves(leads[sub] * eye - maps[DV:])
+
+        @pl.when(g >= ahead)
         def _():
-            copy.wait_recv()
-
-        @pl.when(jnp.logical_not(not_first))
+            pass_state(g - ahead)
+
+        return carry
+
+    lax.fori_loop(0, heads_k, key_side, 0)
+
+    def query_side(g, carry):
+        query = unit(conv(g * DK, taps_query_key.at[0], g * DK)) * DK ** (-0.5)
+        query_dot = mm(query.astype(BF16), keys[:, head_lanes(g)], ((1,), (1,)))
+        firsts, edges = [], []
+        for sub in range(repeat):
+            h = g * repeat + sub
+            lead = jnp.exp(column(gam_ref[pl.ds(h, 1), :])) * enters
+            both = mm((query_dot * decays[h]).astype(BF16), corrected[h])
+            firsts.append(both[:, :DV])
+            edges.append((lead * query - both[:, DV:]).astype(BF16))
+
+        @pl.when(g >= heads_k - ahead)
         def _():
-            incoming[h] = jnp.zeros((DV, DK), BF16)
-
-        state = incoming[h]
-
-        @pl.when(not_last)
-        def _():
-            map_high, map_low = halves(mmat[h])
-            outgoing[h] = (mm(state, map_high) + mm(state, map_low) + bmat[h]).astype(BF16)
-            copy.start()
-
-        lanes = pl.ds(pl.multiple_of(h * DV, 128), DV)
-        recur = local_out[:, lanes] + mm(edge[:, lanes], state, ((1,), (1,)))
-        scale = lax.rsqrt(jnp.mean(recur * recur, axis=-1, keepdims=True) + 1e-06)
-        normed[:, lanes] = (recur * scale * gain_ref[...] * silu(gate_ref[:, lanes])).astype(BF16)
-        return carry
-
-    lax.fori_loop(0, heads_v, chain, 0)
+            pass_state(g)
+
+        for sub in range(repeat):
+            lanes = head_lanes(g * repeat + sub)
+            state = incoming[g, sub * DV : (sub + 1) * DV, :]
+            recur = firsts[sub] + mm(edges[sub], state, ((1,), (1,)))
+            scale = lax.rsqrt(jnp.mean(recur * recur, axis=-1, keepdims=True) + 1e-06)
+            normed[:, lanes] = (recur * scale * gain_ref[...] * silu(gate_ref[:, lanes])).astype(BF16)
+        return carry
+
+    lax.fori_loop(0, heads_k, query_side, 0)
 
     loads[3].wait()
     tiles = depth // OUT_TILE
@@ -408,18 +436,11 @@
     def _():
         tail_copy.wait_send()
 
-        def drain(h, carry):
-            pltpu.make_async_remote_copy(
-                src_ref=outgoing.at[h],
-                dst_ref=incoming.at[h],
-                send_sem=send_sems.at[h],
-                recv_sem=recv_sems.at[h],
-                device_id={"ctx": me + 1},
-                device_id_type=MESH,
-            ).wait_send()
+        def drain(g, carry):
+            state_copy(g).wait_send()
             return carry
 
-        lax.fori_loop(0, heads_v, drain, 0)
+        lax.fori_loop(0, heads_k, drain, 0)
 
 
 def local(
@@ -447,14 +468,13 @@
     chips = peers // 2
     others = max(chips - 1, 1)
     tiles = depth // OUT_TILE
-    taps = jnp.concatenate([conv_query_key[0], conv_query_key[1], conv_value], axis=1)
     vmem = pl.BlockSpec(memory_space=pltpu.VMEM)
     anywhere = pl.BlockSpec(memory_space=pl.ANY)
     dma = pltpu.SemaphoreType.DMA
     return pl.pallas_call(
         functools.partial(layer, devices, peers, heads_v // heads_k),
         out_shape=jax.ShapeDtypeStruct((rows, depth), BF16),
-        in_specs=[vmem] * 6 + [anywhere] * 4,
+        in_specs=[vmem] * 7 + [anywhere] * 4,
         out_specs=vmem,
         scratch_shapes=[
             pltpu.VMEM(w_query_key.shape, BF16),
@@ -469,12 +489,14 @@
             pltpu.VMEM((TAIL, width), BF16),
             pltpu.VMEM((HALF, HALF), jnp.int32),
             pltpu.VMEM((heads_v, count), F32),
-            pltpu.VMEM((count, width_v), F32),
-            pltpu.VMEM((count, width_v), BF16),
-            pltpu.VMEM((heads_v, DK, DK), F32),
+            pltpu.VMEM((count, width_qk), BF16),
+            pltpu.VMEM((heads_v, count, count), F32),
+            pltpu.VMEM((heads_v, count, DV + DK), BF16),
+            pltpu.VMEM((heads_v, DK, DK), BF16),
+            pltpu.VMEM((heads_v, DK, DK), BF16),
             pltpu.VMEM((heads_v, DV, DK), F32),
-            pltpu.VMEM((heads_v, DV, DK), BF16),
-            pltpu.VMEM((heads_v, DV, DK), BF16),
+            pltpu.VMEM((heads_k, heads_v // heads_k * DV, DK), BF16),
+            pltpu.VMEM((heads_k, heads_v // heads_k * DV, DK), BF16),
             pltpu.VMEM((tiles, chips * rows, OUT_TILE), BF16),
             pltpu.VMEM((tiles, chips * rows, OUT_TILE), BF16),
             pltpu.VMEM((tiles, others, rows, OUT_TILE), BF16),
@@ -482,8 +504,8 @@
             pltpu.VMEM((rows, depth), F32),
             dma((4,)),
             dma((2,)),
-            dma((heads_v,)),
-            dma((heads_v,)),
+            dma((heads_k,)),
+            dma((heads_k,)),
             dma((chips,)),
             dma((chips,)),
             dma((chips,)),
@@ -498,7 +520,8 @@
         ),
     )(
         tokens,
-        taps,
+        conv_query_key,
+        conv_value,
         log_decay,
         beta,
         seg_start.reshape(1, count),

time: 91.9 us -> 68.3 us (0.74)
  Pallas kernels: 87.8 us -> 66.5 us
  other arithmetic: 1.34 us -> 0 us
    pallas_call x1, Pallas kernels: 87.8 us -> 66.5 us  [local(): pl.pallas_call(functools.partial(layer, devices, peers, heads_v // heads_...]
    concatenate x1 -> x0, other arithmetic: 1.34 us -> none  [local(): jnp.concatenate([conv_query_key[0], conv_query_key[1], conv_value], axis=1)]
where the time goes in v3:
time: 68.3 us; the launch traced here: 68.2 us
  Pallas kernels  66.5 us (97%)
  local copies, waits for them, and re-layouts  1.67 us (2%)
    pallas_call x1, Pallas kernels, local(): pl.pallas_call(functools.partial(layer, devices, peers, heads_v // heads_...  66.5 us
    unnamed x1, local copies, waits for them, and re-layouts  1.67 us

profile of v3, /device:TPU:26, one launch (start us, length us, event | category | flops | bytes accessed | tf_op | source)
XLA Modules:
  0.0 68.2 jit_solution(6216597154090206609)
XLA Ops:
  0.0 66.5 %shard_map.109 = bf16[64,2048]{1,0:T(8,128)(2,1)} custom-call(bf16[64,2048]{1,0:T(8,128)(2,1)} %tokens_ref.1, f32[2,4,512]{2,1,0:T(4,128)} %taps_query_key.1, f32[4,1024]{1,0:T(4,128)} %taps_value.1, f32[8,256]{1,0:T(8,128)} %logd_ref.1, f32[8,256]{1,0:T(8,128)} %beta_ref.1, s32[1,256]{1,0:T(1,128)} %bitcast.2, f32[1,128]{1,0:T(1,128)} %bitcast.3, ...), custom_call_target="tpu_custom_call" | custom-call | tf_op jit(solution)/shard_map/pallas_call | solution.py:474
  66.5 1.7 %copy.13 = bf16[64,2048]{1,0:T(8,128)(2,1)} copy(bf16[64,2048]{1,0:T(8,128)(2,1)} %shard_map.109) | data formatting | bytes 524288

commit v4 on v3

--- a/solution.py
+++ b/solution.py
@@ -104,6 +104,11 @@
     bmat,
     outgoing,
     incoming,
+    entering,
+    maps_out,
+    maps_in,
+    leads_out,
+    leads_in,
     core_out,
     core_in,
     chip_out,
@@ -113,6 +118,11 @@
     tail_sems,
     send_sems,
     recv_sems,
+    far_send,
+    maps_send,
+    maps_recv,
+    leads_send,
+    leads_recv,
     gather_send,
     gather_recv,
     pass_send,
@@ -128,6 +138,11 @@
     partner = chip * 2 + 1 - core
     not_first = me > 0
     not_last = me < devices - 1
+    pair = me // 2
+    odd = me % 2 == 1
+    even = me % 2 == 0
+    has_before = jnp.logical_and(odd, me > 2)
+    has_after = jnp.logical_and(odd, not_last)
     rows, depth = tokens_ref.shape
     count = rows * peers
     heads_v = logd_ref.shape[0]
@@ -166,10 +181,20 @@
     def _():
         pl.semaphore_signal(barrier, inc=1, device_id={"ctx": me + 1}, device_id_type=MESH)
 
+    @pl.when(has_before)
+    def _():
+        pl.semaphore_signal(barrier, inc=1, device_id={"ctx": me - 2}, device_id_type=MESH)
+
+    @pl.when(has_after)
+    def _():
+        pl.semaphore_signal(barrier, inc=1, device_id={"ctx": me + 2}, device_id_type=MESH)
+
     pl.semaphore_signal(barrier, inc=1, device_id={"tp": partner}, device_id_type=MESH)
     for d in range(1, chips):
         pl.semaphore_signal(barrier, inc=1, device_id=on_chip(d), device_id_type=MESH)
-    pl.semaphore_wait(barrier, not_first.astype(jnp.int32) + not_last.astype(jnp.int32) + chips)
+    near = not_first.astype(jnp.int32) + not_last.astype(jnp.int32)
+    far = has_before.astype(jnp.int32) + has_after.astype(jnp.int32)
+    pl.semaphore_wait(barrier, near + far + chips)
 
     def remote(src, dst, send, recv, device):
         return pltpu.make_async_remote_copy(
@@ -268,31 +293,70 @@
     def unit(x):
         return x * lax.rsqrt(jnp.sum(x * x, axis=-1, keepdims=True) + 1e-06)
 
-    def state_copy(g):
+    def to_next(g):
         return remote(outgoing.at[g], incoming.at[g], send_sems.at[g], recv_sems.at[g], {"ctx": me + 1})
+
+    def to_pair(g):
+        return remote(outgoing.at[g], incoming.at[g], far_send.at[g], recv_sems.at[g], {"ctx": me + 2})
+
+    def map_copies(g):
+        to = {"ctx": me + 1}
+        return (
+            remote(maps_out.at[g], maps_in.at[g], maps_send.at[g], maps_recv.at[g], to),
+            remote(leads_out.at[g], leads_in.at[g], leads_send.at[g], leads_recv.at[g], to),
+        )
 
     def head_lanes(h):
         return pl.ds(pl.multiple_of(h * DV, 128), DV)
 
+    span = DV + DK
+
+    def join_maps(g):
+        for copy in map_copies(g):
+            copy.wait_recv()
+        for sub in range(repeat):
+            h = g * repeat + sub
+            high, low = map_high[h], map_low[h]
+            slab = maps_in[g, sub * span : (sub + 1) * span, :]
+            product = mm(slab, high) + mm(slab, low)
+            bmat[h] = bmat[h] + product[:DV]
+            lead = leads_in[g, sub : sub + 1, :]
+            map_high[h], map_low[h] = halves(lead * (high.astype(F32) + low.astype(F32)) - product[DV:])
+
     def pass_state(g):
-        @pl.when(not_first)
-        def _():
-            state_copy(g).wait_recv()
-
-        @pl.when(jnp.logical_not(not_first))
+        @pl.when(pair > 0)
+        def _():
+            to_next(g).wait_recv()
+
+        @pl.when(pair == 0)
         def _():
             incoming[g] = jnp.zeros((repeat * DV, DK), BF16)
 
-        @pl.when(not_last)
+        @pl.when(has_after)
         def _():
             for sub in range(repeat):
                 h = g * repeat + sub
                 part = slice(sub * DV, (sub + 1) * DV)
                 state = incoming[g, part, :]
                 outgoing[g, part, :] = (mm(state, map_high[h]) + mm(state, map_low[h]) + bmat[h]).astype(BF16)
-            state_copy(g).start()
-
-    ahead = jnp.minimum(me, heads_k)
+            to_pair(g).start()
+            to_next(g).start()
+
+        @pl.when(odd)
+        def _():
+            for sub in range(repeat):
+                part = slice(sub * DV, (sub + 1) * DV)
+                state = incoming[g, part, :]
+                b_slab = maps_in[g, sub * span : sub * span + DV, :]
+                m_slab = maps_in[g, sub * span + DV : (sub + 1) * span, :]
+                kept = leads_in[g, sub : sub + 1, :] * state.astype(F32)
+                entering[g, part, :] = (kept - mm(state, m_slab) + b_slab.astype(F32)).astype(BF16)
+
+        @pl.when(even)
+        def _():
+            entering[g] = incoming[g]
+
+    ahead = jnp.minimum(jnp.where(odd, 1 + pair, heads_k), heads_k)
     eye = (iota((HALF, HALF), 0) == iota((HALF, HALF), 1)).astype(F32)
     parts = [slice(b * HALF, (b + 1) * HALF) for b in range(count // HALF)]
 
@@ -335,6 +399,17 @@
             maps = mm((w_both * lasts[sub]).astype(BF16), key_b, ((0,), (0,)))
             bmat[h] = maps[:DV]
             map_high[h], map_low[h] = halves(leads[sub] * eye - maps[DV:])
+            maps_out[g, sub * span : (sub + 1) * span, :] = maps.astype(BF16)
+            leads_out[g, sub : sub + 1, :] = jnp.broadcast_to(leads[sub], (1, DK))
+
+        @pl.when(even)
+        def _():
+            for copy in map_copies(g):
+                copy.start()
+
+        @pl.when(jnp.logical_and(odd, g >= 1))
+        def _():
+            join_maps(g - 1)
 
         @pl.when(g >= ahead)
         def _():
@@ -343,6 +418,10 @@
         return carry
 
     lax.fori_loop(0, heads_k, key_side, 0)
+
+    @pl.when(odd)
+    def _():
+        join_maps(heads_k - 1)
 
     def query_side(g, carry):
         query = unit(conv(g * DK, taps_query_key.at[0], g * DK)) * DK ** (-0.5)
@@ -361,7 +440,7 @@
 
         for sub in range(repeat):
             lanes = head_lanes(g * repeat + sub)
-            state = incoming[g, sub * DV : (sub + 1) * DV, :]
+            state = entering[g, sub * DV : (sub + 1) * DV, :]
             recur = firsts[sub] + mm(edges[sub], state, ((1,), (1,)))
             scale = lax.rsqrt(jnp.mean(recur * recur, axis=-1, keepdims=True) + 1e-06)
             normed[:, lanes] = (recur * scale * gain_ref[...] * silu(gate_ref[:, lanes])).astype(BF16)
@@ -436,8 +515,20 @@
     def _():
         tail_copy.wait_send()
 
+    @pl.when(has_after)
+    def _():
         def drain(g, carry):
-            state_copy(g).wait_send()
+            to_pair(g).wait_send()
+            to_next(g).wait_send()
+            return carry
+
+        lax.fori_loop(0, heads_k, drain, 0)
+
+    @pl.when(even)
+    def _():
+        def drain(g, carry):
+            for copy in map_copies(g):
+                copy.wait_send()
             return carry
 
         lax.fori_loop(0, heads_k, drain, 0)
@@ -497,6 +588,11 @@
             pltpu.VMEM((heads_v, DV, DK), F32),
             pltpu.VMEM((heads_k, heads_v // heads_k * DV, DK), BF16),
             pltpu.VMEM((heads_k, heads_v // heads_k * DV, DK), BF16),
+            pltpu.VMEM((heads_k, heads_v // heads_k * DV, DK), BF16),
+            pltpu.VMEM((heads_k, heads_v // heads_k * (DV + DK), DK), BF16),
+            pltpu.VMEM((heads_k, heads_v // heads_k * (DV + DK), DK), BF16),
+            pltpu.VMEM((heads_k, 8, DK), F32),
+            pltpu.VMEM((heads_k, 8, DK), F32),
             pltpu.VMEM((tiles, chips * rows, OUT_TILE), BF16),
             pltpu.VMEM((tiles, chips * rows, OUT_TILE), BF16),
             pltpu.VMEM((tiles, others, rows, OUT_TILE), BF16),
@@ -504,6 +600,11 @@
             pltpu.VMEM((rows, depth), F32),
             dma((4,)),
             dma((2,)),
+            dma((heads_k,)),
+            dma((heads_k,)),
+            dma((heads_k,)),
+            dma((heads_k,)),
+            dma((heads_k,)),
             dma((heads_k,)),
             dma((heads_k,)),
             dma((chips,)),

time: 68.3 us -> 63 us (0.922)
  the two profiles are of different devices: /device:TPU:26 before, /device:TPU:24 now
where the time goes in v4:
time: 63 us; the launch traced here: 62.8 us
  Pallas kernels  61.1 us (97%)
  local copies, waits for them, and re-layouts  1.67 us (3%)
    pallas_call x1, Pallas kernels, local(): pl.pallas_call(functools.partial(layer, devices, peers, heads_v // heads_...  61.1 us
    unnamed x1, local copies, waits for them, and re-layouts  1.67 us

profile of v4, /device:TPU:24, one launch (start us, length us, event | category | flops | bytes accessed | tf_op | source)
XLA Modules:
  0.0 62.8 jit_solution(11124204364387056286)
XLA Ops:
  0.0 61.1 %shard_map.109 = bf16[64,2048]{1,0:T(8,128)(2,1)} custom-call(bf16[64,2048]{1,0:T(8,128)(2,1)} %tokens_ref.1, f32[2,4,512]{2,1,0:T(4,128)} %taps_query_key.1, f32[4,1024]{1,0:T(4,128)} %taps_value.1, f32[8,256]{1,0:T(8,128)} %logd_ref.1, f32[8,256]{1,0:T(8,128)} %beta_ref.1, s32[1,256]{1,0:T(1,128)} %bitcast.2, f32[1,128]{1,0:T(1,128)} %bitcast.3, ...), custom_call_target="tpu_custom_call" | custom-call | tf_op jit(solution)/shard_map/pallas_call | solution.py:565
  61.1 1.7 %copy.13 = bf16[64,2048]{1,0:T(8,128)(2,1)} copy(bf16[64,2048]{1,0:T(8,128)(2,1)} %shard_map.109) | data formatting | bytes 524288

commit v5 on v4

--- a/solution.py
+++ b/solution.py
@@ -142,6 +142,8 @@
     odd = me % 2 == 1
     even = me % 2 == 0
     has_before = jnp.logical_and(odd, me > 2)
+    forwards = jnp.logical_and(odd, pair > 0)
+    opens = jnp.logical_and(odd, pair == 0)
     has_after = jnp.logical_and(odd, not_last)
     rows, depth = tokens_ref.shape
     count = rows * peers
@@ -293,8 +295,8 @@
     def unit(x):
         return x * lax.rsqrt(jnp.sum(x * x, axis=-1, keepdims=True) + 1e-06)
 
-    def to_next(g):
-        return remote(outgoing.at[g], incoming.at[g], send_sems.at[g], recv_sems.at[g], {"ctx": me + 1})
+    def to_even(g):
+        return remote(incoming.at[g], incoming.at[g], send_sems.at[g], recv_sems.at[g], {"ctx": me - 1})
 
     def to_pair(g):
         return remote(outgoing.at[g], incoming.at[g], far_send.at[g], recv_sems.at[g], {"ctx": me + 2})
@@ -326,7 +328,11 @@
     def pass_state(g):
         @pl.when(pair > 0)
         def _():
-            to_next(g).wait_recv()
+            to_pair(g).wait_recv()
+
+        @pl.when(forwards)
+        def _():
+            to_even(g).start()
 
         @pl.when(pair == 0)
         def _():
@@ -340,7 +346,6 @@
                 state = incoming[g, part, :]
                 outgoing[g, part, :] = (mm(state, map_high[h]) + mm(state, map_low[h]) + bmat[h]).astype(BF16)
             to_pair(g).start()
-            to_next(g).start()
 
         @pl.when(odd)
         def _():
@@ -423,6 +428,10 @@
     def _():
         join_maps(heads_k - 1)
 
+    @pl.when(opens)
+    def _():
+        pass_state(heads_k - 1)
+
     def query_side(g, carry):
         query = unit(conv(g * DK, taps_query_key.at[0], g * DK)) * DK ** (-0.5)
         query_dot = mm(query.astype(BF16), keys[:, head_lanes(g)], ((1,), (1,)))
@@ -434,9 +443,9 @@
             firsts.append(both[:, :DV])
             edges.append((lead * query - both[:, DV:]).astype(BF16))
 
-        @pl.when(g >= heads_k - ahead)
-        def _():
-            pass_state(g)
+        @pl.when(jnp.logical_and(g < ahead, jnp.logical_not(opens)))
+        def _():
+            pass_state(heads_k - ahead + g)
 
         for sub in range(repeat):
             lanes = head_lanes(g * repeat + sub)
@@ -519,7 +528,14 @@
     def _():
         def drain(g, carry):
             to_pair(g).wait_send()
-            to_next(g).wait_send()
+            return carry
+
+        lax.fori_loop(0, heads_k, drain, 0)
+
+    @pl.when(forwards)
+    def _():
+        def drain(g, carry):
+            to_even(g).wait_send()
             return carry
 
         lax.fori_loop(0, heads_k, drain, 0)

time: 63 us -> 61.8 us (0.981)
  Pallas kernels: 61.1 us -> 59.9 us
    pallas_call x1, Pallas kernels: 61.1 us -> 59.9 us  [local(): pl.pallas_call(functools.partial(layer, devices, peers, heads_v // heads_...]
where the time goes in v5:
time: 61.8 us; the launch traced here: 61.6 us
  Pallas kernels  59.9 us (97%)
  local copies, waits for them, and re-layouts  1.67 us (3%)
    pallas_call x1, Pallas kernels, local(): pl.pallas_call(functools.partial(layer, devices, peers, heads_v // heads_...  59.9 us
    unnamed x1, local copies, waits for them, and re-layouts  1.67 us

profile of v5, /device:TPU:24, one launch (start us, length us, event | category | flops | bytes accessed | tf_op | source)
XLA Modules:
  0.0 61.6 jit_solution(14943348668540964843)
XLA Ops:
  0.0 59.9 %shard_map.109 = bf16[64,2048]{1,0:T(8,128)(2,1)} custom-call(bf16[64,2048]{1,0:T(8,128)(2,1)} %tokens_ref.1, f32[2,4,512]{2,1,0:T(4,128)} %taps_query_key.1, f32[4,1024]{1,0:T(4,128)} %taps_value.1, f32[8,256]{1,0:T(8,128)} %logd_ref.1, f32[8,256]{1,0:T(8,128)} %beta_ref.1, s32[1,256]{1,0:T(1,128)} %bitcast.2, f32[1,128]{1,0:T(1,128)} %bitcast.3, ...), custom_call_target="tpu_custom_call" | custom-call | tf_op jit(solution)/shard_map/pallas_call | solution.py:581
  59.9 1.7 %copy.13 = bf16[64,2048]{1,0:T(8,128)(2,1)} copy(bf16[64,2048]{1,0:T(8,128)(2,1)} %shard_map.109) | data formatting | bytes 524288

commit v6 on v4

--- a/solution.py
+++ b/solution.py
@@ -142,6 +142,7 @@
     odd = me % 2 == 1
     even = me % 2 == 0
     has_before = jnp.logical_and(odd, me > 2)
+    opens = jnp.logical_and(odd, pair == 0)
     has_after = jnp.logical_and(odd, not_last)
     rows, depth = tokens_ref.shape
     count = rows * peers
@@ -326,7 +327,7 @@
     def pass_state(g):
         @pl.when(pair > 0)
         def _():
-            to_next(g).wait_recv()
+            to_pair(g).wait_recv()
 
         @pl.when(pair == 0)
         def _():
@@ -423,6 +424,10 @@
     def _():
         join_maps(heads_k - 1)
 
+    @pl.when(opens)
+    def _():
+        pass_state(heads_k - 1)
+
     def query_side(g, carry):
         query = unit(conv(g * DK, taps_query_key.at[0], g * DK)) * DK ** (-0.5)
         query_dot = mm(query.astype(BF16), keys[:, head_lanes(g)], ((1,), (1,)))
@@ -434,9 +439,9 @@
             firsts.append(both[:, :DV])
             edges.append((lead * query - both[:, DV:]).astype(BF16))
 
-        @pl.when(g >= heads_k - ahead)
-        def _():
-            pass_state(g)
+        @pl.when(jnp.logical_and(g < ahead, jnp.logical_not(opens)))
+        def _():
+            pass_state(heads_k - ahead + g)
 
         for sub in range(repeat):
             lanes = head_lanes(g * repeat + sub)

time: 63 us -> 61.1 us (0.970)
  Pallas kernels: 61.1 us -> 59.2 us
    pallas_call x1, Pallas kernels: 61.1 us -> 59.2 us  [local(): pl.pallas_call(functools.partial(layer, devices, peers, heads_v // heads_...]
where the time goes in v6:
time: 61.1 us; the launch traced here: 60.9 us
  Pallas kernels  59.2 us (97%)
  local copies, waits for them, and re-layouts  1.67 us (3%)
    pallas_call x1, Pallas kernels, local(): pl.pallas_call(functools.partial(layer, devices, peers, heads_v // heads_...  59.2 us
    unnamed x1, local copies, waits for them, and re-layouts  1.67 us

profile of v6, /device:TPU:24, one launch (start us, length us, event | category | flops | bytes accessed | tf_op | source)
XLA Modules:
  0.0 60.9 jit_solution(16658100670172040308)
XLA Ops:
  0.0 59.2 %shard_map.109 = bf16[64,2048]{1,0:T(8,128)(2,1)} custom-call(bf16[64,2048]{1,0:T(8,128)(2,1)} %tokens_ref.1, f32[2,4,512]{2,1,0:T(4,128)} %taps_query_key.1, f32[4,1024]{1,0:T(4,128)} %taps_value.1, f32[8,256]{1,0:T(8,128)} %logd_ref.1, f32[8,256]{1,0:T(8,128)} %beta_ref.1, s32[1,256]{1,0:T(1,128)} %bitcast.2, f32[1,128]{1,0:T(1,128)} %bitcast.3, ...), custom_call_target="tpu_custom_call" | custom-call | tf_op jit(solution)/shard_map/pallas_call | solution.py:570
  59.3 1.7 %copy.13 = bf16[64,2048]{1,0:T(8,128)(2,1)} copy(bf16[64,2048]{1,0:T(8,128)(2,1)} %shard_map.109) | data formatting | bytes 524288
